TPU v7x, 32 devices: a whole 2x2x4 slice. The times are simulated.
32 devices in a mesh: dp: 8 (over z, x), mp: 4 (over y, core).
Axes of the slice: x: 2, y: 2, z: 4, core: 2. Of those that a mesh axis runs over, the one named last changes fastest.
Arguments:
- token_ids: int32 [512, 7], replicated, may hold values from 0 to 65535
- lengths: int32 [512], replicated, may hold values from 1 to 7, as said below
- pack_dest: int32 [512], replicated, may hold values from 0 to 7, as said below
- ref_hidden: bfloat16 [512, 7, 4096], P('dp', None, 'mp'), may hold values from -45 to 45
- reward_hidden: bfloat16 [512, 7, 4096], P('dp', None, 'mp'), may hold values from -140 to 140
- head_weight: bfloat16 [4096, 65536], P('mp', 'dp'), may hold values from -0.25 to 0.25
- norm_gain: float32 [4096], P('mp'), may hold values from 0.1 to 1.9
- score_weight: float32 [4096], P('mp'), may hold values from -0.09375 to 0.09375
- value_weight: float32 [4096], P('mp'), may hold values from -0.09375 to 0.09375
- old_logprob: float32 [2048], P('dp'), may hold values from -14 to -1
Outputs:
- ref_logprob: float32 [2048], P('dp')
- advantage: float32 [2048], P('dp')
Inputs may be any that keep to these rules, and one draw needn't show every extreme that they name: `pack_dest`: request i belongs to request shard i // 64. Each request shard sends exactly 8 of its requests to every packed shard. A packed shard lists its requests by request shard, then by request index, and packs their tokens in that order from slot 0. In that order the requests of a packed shard form pairs whose lengths sum to 8, so every packed shard holds exactly 256 tokens; every packed shard has a request of length 1 and one of length 7.
All inputs are finite; a program needn't handle non-finite values.
Results may differ from a plain program's by a relative error of at most 0.0003.
Values may be sent and summed in bfloat16 or wider, within the bound.
A program may use at most 192 MiB of HBM per device.

v0:
```python
import math

import jax
import jax.numpy as jnp
from jax import lax
from jax.sharding import PartitionSpec as P

kl_coef = 0.1
discount = 0.99
gae_mix = 0.95
norm_eps = 1e-05


def combined_all(part, axis, combine):
    gathered = jax.tree.map(lambda a: lax.all_gather(a, axis), part)

    def take(source):
        return jax.tree.map(lambda a: lax.dynamic_index_in_dim(a, source, 0, False), gathered)

    return lax.fori_loop(
        1, lax.axis_size(axis), lambda source, state: combine(state, take(source)), take(0)
    )


def pack_tables(pack_dest, lengths, shards, req_dev, slot_dev):
    per_pair = req_dev // shards
    target_shard = pack_dest.reshape(shards, req_dev)
    same_shard = target_shard[:, :, None] == target_shard[:, None, :]
    earlier = (
        jnp.arange(req_dev, dtype=jnp.int32)[None, :]
        < jnp.arange(req_dev, dtype=jnp.int32)[:, None]
    )
    rank_in = jnp.sum(jnp.logical_and(same_shard, earlier[None]).astype(jnp.int32), axis=2)
    packed_pos = jnp.arange(shards, dtype=jnp.int32)[:, None] * per_pair + rank_in
    packed_place = (target_shard * req_dev + packed_pos).reshape(-1)
    source_of = (
        jnp.zeros((shards * req_dev,), jnp.int32)
        .at[packed_place]
        .set(jnp.arange(shards * req_dev, dtype=jnp.int32))
        .reshape(shards, req_dev)
    )
    packed_len = lengths[source_of]
    offsets = jnp.cumsum(packed_len, axis=1, dtype=jnp.int32) - packed_len
    slot_ids = jnp.arange(slot_dev, dtype=jnp.int32)
    request_at = (
        jnp.sum((offsets[:, None, :] <= slot_ids[None, :, None]).astype(jnp.int32), axis=2) - 1
    )
    start_at = jnp.take_along_axis(offsets, request_at, axis=1)
    offset_in = slot_ids[None, :] - start_at
    is_last = offset_in == jnp.take_along_axis(packed_len, request_at, axis=1) - 1
    source_prompt = jnp.take_along_axis(source_of, request_at, axis=1)
    return (target_shard, packed_pos, request_at, offset_in, is_last, source_prompt)


def advantages(reward, value_est, is_last, request_at):
    slot_count = reward.shape[0]
    next_value = jnp.concatenate([value_est[1:], jnp.zeros((1,), jnp.float32)])
    not_last = 1.0 - is_last.astype(jnp.float32)
    td_error = reward + discount * next_value * not_last - value_est
    slot_ids = jnp.arange(slot_count, dtype=jnp.int32)
    step_gap = (slot_ids[None, :] - slot_ids[:, None]).astype(jnp.float32)
    same_req = jnp.logical_and(request_at[:, None] == request_at[None, :], step_gap >= 0)
    weights = jnp.where(
        same_req, jnp.exp(jnp.maximum(step_gap, 0.0) * math.log(discount * gae_mix)), 0.0
    )
    return jnp.dot(weights, td_error, precision=lax.Precision.HIGHEST)


def combine_softmax(left_part, right_part):
    joint_max = jnp.maximum(left_part[0], right_part[0])
    joint_total = left_part[1] * jnp.exp(left_part[0] - joint_max) + right_part[1] * jnp.exp(
        right_part[0] - joint_max
    )
    return (joint_max, joint_total, left_part[2] + right_part[2])


def body(
    token_ids,
    lengths,
    pack_dest,
    ref_hidden,
    reward_hidden,
    head_weight,
    norm_gain,
    score_weight,
    value_weight,
    old_logprob,
):
    shards = lax.axis_size("dp")
    tensor_ways = lax.axis_size("mp")
    shard_index = lax.axis_index("dp")
    part_index = lax.axis_index("mp")
    req_dev, max_len, width_dev = ref_hidden.shape
    slot_dev = req_dev // 2 * (max_len + 1)
    sub_len = slot_dev // tensor_ways
    per_pair = req_dev // shards
    target_shard, packed_pos, request_at, offset_in, is_last, source_prompt = pack_tables(
        pack_dest, lengths, shards, req_dev, slot_dev
    )
    my_shards = lax.dynamic_index_in_dim(target_shard, shard_index, 0, keepdims=False)
    my_rank = (
        lax.dynamic_index_in_dim(packed_pos, shard_index, 0, keepdims=False)
        - shard_index * per_pair
    )
    send_place = my_shards * per_pair + my_rank
    send_order = (
        jnp.zeros((req_dev,), jnp.int32).at[send_place].set(jnp.arange(req_dev, dtype=jnp.int32))
    )
    ref_send = jnp.take(ref_hidden, send_order, axis=0).reshape(
        shards, per_pair * max_len, width_dev
    )
    reward_send = jnp.take(reward_hidden, send_order, axis=0).reshape(
        shards, per_pair * max_len, width_dev
    )
    ref_got, reward_got = (
        lax.all_to_all(ref_send, "dp", split_axis=0, concat_axis=0, tiled=True),
        lax.all_to_all(reward_send, "dp", split_axis=0, concat_axis=0, tiled=True),
    )
    my_request = lax.dynamic_index_in_dim(request_at, shard_index, 0, keepdims=False)
    my_offset = lax.dynamic_index_in_dim(offset_in, shard_index, 0, keepdims=False)
    my_last = lax.dynamic_index_in_dim(is_last, shard_index, 0, keepdims=False)
    row_index = my_request * max_len + my_offset
    ref_packed = jnp.take(ref_got.reshape(req_dev * max_len, width_dev), row_index, axis=0)
    reward_packed = jnp.take(reward_got.reshape(req_dev * max_len, width_dev), row_index, axis=0)
    all_targets = token_ids.reshape(-1)[(source_prompt * max_len + offset_in).reshape(-1)].reshape(
        shards, slot_dev
    )
    target_order = jnp.transpose(
        all_targets.reshape(shards, tensor_ways, sub_len), (1, 0, 2)
    ).reshape(-1)
    my_targets = lax.dynamic_index_in_dim(
        target_order.reshape(tensor_ways, -1), part_index, 0, keepdims=False
    )
    vocab_dev = head_weight.shape[1]
    vocab_base = shard_index * vocab_dev
    own_rows = lax.all_to_all(
        ref_packed.reshape(tensor_ways, sub_len, width_dev),
        "mp",
        split_axis=0,
        concat_axis=2,
        tiled=True,
    )
    block_rows = lax.all_gather(own_rows, "dp", axis=0, tiled=True).reshape(
        -1, width_dev * tensor_ways
    )
    logits = jnp.dot(
        block_rows,
        lax.all_gather(head_weight, "mp", axis=0, tiled=True),
        preferred_element_type=jnp.float32,
    )
    row_max = jnp.max(logits, axis=1)
    exp_total = jnp.sum(jnp.exp(logits - row_max[:, None]), axis=1)
    matches = jnp.arange(vocab_dev, dtype=jnp.int32)[None, :] + vocab_base == my_targets[:, None]
    target_logit = jnp.sum(jnp.where(matches, logits, 0.0), axis=1)
    row_max, exp_total, target_logit = combined_all(
        (row_max, exp_total, target_logit), "dp", combine_softmax
    )
    block_logprob = (target_logit - row_max - jnp.log(exp_total)).reshape(shards, sub_len)
    own_block = lax.dynamic_index_in_dim(block_logprob, shard_index, 0, keepdims=False)
    ref_logprob = lax.all_gather(own_block, "mp", axis=0, tiled=True)
    width_full = width_dev * tensor_ways
    hidden_f = reward_packed.astype(jnp.float32)
    squares = lax.psum(jnp.sum(hidden_f * hidden_f, axis=1), "mp")
    inv_rms = lax.rsqrt(squares / width_full + norm_eps)
    normed = hidden_f * inv_rms[:, None] * norm_gain
    score, value_est = lax.psum(
        (jnp.sum(normed * score_weight, axis=1), jnp.sum(normed * value_weight, axis=1)), "mp"
    )
    reward = -kl_coef * (old_logprob - ref_logprob) + jnp.where(my_last, score, 0.0)
    advantage = advantages(reward, value_est, my_last, my_request)
    return (ref_logprob, advantage)


def solution(mesh):
    return jax.shard_map(
        body,
        mesh=mesh,
        in_specs=(
            P(),
            P(),
            P(),
            P("dp", None, "mp"),
            P("dp", None, "mp"),
            P("mp", "dp"),
            P("mp"),
            P("mp"),
            P("mp"),
            P("dp"),
        ),
        out_specs=(P("dp"), P("dp")),
        check_vma=False,
    )
```

profile of v0, /device:TPU:0, one launch (start us, length us, event | category | flops | bytes accessed | tf_op | source)
XLA Modules:
  0.0 702.9 jit_solution(16059098734433597331)
XLA Ops:
  7.2 0.8 reshape.192
  8.5 0.8 scatter_custom_fusion
  9.3 3.2 gather_fusion.7
  12.6 3.4 gather_fusion.2
  16.0 1.2 broadcast_select_fusion
  17.7 1.2 reshape.193
  19.0 7.2 %all-to-all-start = ((bf16[8,56,1024]{2,1,0:T(8,128)(2,1)}), bf16[8,56,1024]{2,1,0:T(8,128)(2,1)S(1)}, u32[]{:S(2)}, u32[]{:S(2)}) async-start(bf16[8,56,1024]{2,1,0:T(8,128)(2,1)} %reshape.193), calls=%async_computation | async-start | bytes 1835008 | tf_op jit(solution)/shard_map/all_to_all | solution.py:116
  26.3 2.4 scatter_custom_fusion.1
  29.0 3.5 gather_fusion
  33.0 9.1 %gather_fusion.6 = s32[2048]{0:T(1024)S(1)} fusion(s32[8,64]{1,0:T(8,128)S(1)} %reshape.257, s32[2048]{0:T(1024)S(1)} %bitcast.71), kind=kCustom, calls=%fused_computation.5.clone | custom fusion | bytes 32768 | tf_op jit(solution)/shard_map/jit(take_along_axis)/gather | solution.py:50
  42.1 9.1 %gather_fusion.3 = s32[2048]{0:T(1024)S(1)} fusion(s32[8,64]{1,0:T(8,128)S(1)} %sub.102, s32[2048]{0:T(1024)S(1)} %bitcast.72), kind=kCustom, calls=%fused_computation.1.clone | custom fusion | bytes 32768 | tf_op jit(solution)/shard_map/jit(take_along_axis)/gather | solution.py:48
  51.3 9.1 %gather_fusion.5 = s32[2048]{0:T(1024)S(1)} fusion(s32[8,64]{1,0:T(8,128)S(1)} %reshape.199, s32[2048]{0:T(1024)S(1)} %bitcast.73), kind=kCustom, calls=%fused_computation.4.clone | custom fusion | bytes 32768 | tf_op jit(solution)/shard_map/jit(take_along_axis)/gather | solution.py:51
  60.6 1.2 gather_fusion.4
  61.9 11.4 %all_to_all.28 = bf16[4,64,1024]{2,1,0:T(8,128)(2,1)S(1)} all-to-all(bf16[4,64,1024]{2,1,0:T(8,128)(2,1)S(1)} %bitcast.77), channel_id=1, replica_groups=mesh['dp'=8,'mp'=4] {'mp'}, dimensions={0} | all-to-all | bytes 1048576 | tf_op jit(solution)/shard_map/all_to_all | solution.py:136
  73.4 0.8 copy.34
  74.3 0.7 all-gather.12.cloned.1.call-update
  75.5 1.2 reshape.202
  76.8 6.0 all-to-all-start.2
  83.1 11.8 %gather_fusion.1 = s32[2048]{0:T(1024)S(1)} fusion(s32[3584]{0:T(1024)S(1)} %reshape.198, s32[2048]{0:T(1024)S(1)} %broadcast_clamp_fusion), kind=kCustom, calls=%fused_computation.8 | custom fusion | bytes 24576 | tf_op jit(solution)/shard_map/gather | solution.py:125
  96.4 25.9 %all-to-all-done.2 = bf16[8,56,1024]{2,1,0:T(8,128)(2,1)S(1)} async-done(((bf16[8,56,1024]{2,1,0:T(8,128)(2,1)}), bf16[8,56,1024]{2,1,0:T(8,128)(2,1)S(1)}, u32[]{:S(2)}, u32[]{:S(2)}) %all-to-all-start.2) | async-done | bytes 917536 | tf_op jit(solution)/shard_map/all_to_all | solution.py:117
  122.3 1.2 gather_fusion.8
  123.7 5.7 psum.21
  129.8 34.8 %all-gather.10.cloned.1.call-done = bf16[8,64,4096]{2,1,0:T(8,128)(2,1)} async-done(((bf16[1,64,4096]{2,1,0:T(8,128)(2,1)}), bf16[8,64,4096]{2,1,0:T(8,128)(2,1)}) %all-gather.10.cloned.1.call-update) | async-done | bytes 4194320 | tf_op jit(solution)/shard_map/all_gather | solution.py:143
  164.7 392.6 %all-gather.12.cloned.1.call-done = bf16[4096,8192]{1,0:T(8,128)(2,1)} async-done(((bf16[1024,8192]{1,0:T(8,128)(2,1)}), bf16[4096,8192]{1,0:T(8,128)(2,1)}) %all-gather.12.cloned.1.call-update) | async-done | bytes 67108880 | tf_op jit(solution)/shard_map/all_gather | solution.py:148
  557.3 44.4 %fusion.36 = (f32[512]{0:T(512)S(1)}, f32[512,8192]{1,0:T(8,128)}) fusion(bf16[512,4096]{1,0:T(8,128)(2,1)} %bitcast.99, bf16[4096,8192]{1,0:T(8,128)(2,1)} %all-gather.12.cloned.1.call-done), kind=kOutput, calls=%fused_computation.100 | convolution fusion | flops 34363932672 | bytes 88082432 | tf_op jit(solution)/shard_map/dot_general | solution.py:146
  601.7 26.2 %all-gather.4 = f32[8,1,512]{2,1,0:T(1,128)S(1)} all-gather(f32[1,1,512]{2,1,0:T(1,128)S(1)} %bitcast.91), channel_id=2, replica_groups=mesh['dp'=8,'mp'=4] {'dp'}, dimensions={0}, use_global_device_ids=true | all-gather | bytes 18432 | tf_op jit(solution)/shard_map/all_gather | solution.py:15
  627.9 8.4 %select_reduce_fusion = (f32[512]{0:T(512)S(1)}, f32[512]{0:T(512)S(1)}) fusion(f32[512,8192]{1,0:T(8,128)} %get-tuple-element.221, s32[8192]{0:T(1024)S(1)} %iota_add_fusion, s32[512]{0:T(512)S(1)} %bitcast.94, f32[512]{0:T(512)S(1)} %get-tuple-element.220), kind=kLoop, calls=%fused_computation.15 | loop fusion | flops 20970496 | bytes 16818176 | tf_op jit(solution)/shard_map/reduce_sum | solution.py:154
  636.3 26.0 %all-gather.5 = f32[8,1,512]{2,1,0:T(1,128)S(1)} all-gather(f32[1,1,512]{2,1,0:T(1,128)S(1)} %bitcast.93), channel_id=3, replica_groups=mesh['dp'=8,'mp'=4] {'dp'}, dimensions={0}, use_global_device_ids=true | all-gather | bytes 18432 | tf_op jit(solution)/shard_map/all_gather | solution.py:15
  662.3 26.0 %all-gather.6 = f32[8,1,512]{2,1,0:T(1,128)S(1)} all-gather(f32[1,1,512]{2,1,0:T(1,128)S(1)} %bitcast.92), channel_id=4, replica_groups=mesh['dp'=8,'mp'=4] {'dp'}, dimensions={0}, use_global_device_ids=true | all-gather | bytes 18432 | tf_op jit(solution)/shard_map/all_gather | solution.py:15
  688.3 0.6 while.19
  689.0 5.9 all-reduce.1
  695.1 1.0 fusion.6
  (115 shorter events, 5.2 us)
Async XLA Ops:
  7.2 2.1 copy-start
  7.2 19.1 %copy-start.4 = (s32[512]{0:T(512)S(1)}, s32[512]{0:T(512)}, u32[]{:S(2)}) copy-start(s32[512]{0:T(512)} %param.20) | copy-start | bytes 6148
  7.2 21.8 %copy-start.1 = (s32[512]{0:T(512)S(1)}, s32[512]{0:T(512)}, u32[]{:S(2)}) copy-start(s32[512]{0:T(512)} %param.19) | copy-start | bytes 6148
  19.0 41.7 %all-to-all-start = ((bf16[8,56,1024]{2,1,0:T(8,128)(2,1)}), bf16[8,56,1024]{2,1,0:T(8,128)(2,1)S(1)}, u32[]{:S(2)}, u32[]{:S(2)}) async-start(bf16[8,56,1024]{2,1,0:T(8,128)(2,1)} %reshape.193), calls=%async_computation | async-start | bytes 1835008 | tf_op jit(solution)/shard_map/all_to_all | solution.py:116
  26.2 138.5 %all-gather.10.cloned.1.call-start = ((), (), s32[]{:S(2)}) async-start(), calls=%async_computation.3 | async-start | bytes 4718592 | tf_op jit(solution)/shard_map/all_gather | solution.py:143
  51.3 23.7 %copy-start.2 = (bf16[64,7,1024]{2,0,1:T(8,128)(2,1)S(1)}, bf16[64,7,1024]{2,0,1:T(8,128)(2,1)}, u32[]{:S(2)}) copy-start(bf16[64,7,1024]{2,0,1:T(8,128)(2,1)} %get-tuple-element.218) | copy-start | bytes 2752516
  60.5 22.3 %copy-start.3 = (s32[512,7]{0,1:T(8,128)S(1)}, s32[512,7]{0,1:T(8,128)}, u32[]{:S(2)}) copy-start(s32[512,7]{0,1:T(8,128)} %param.18) | copy-start | bytes 43012
  73.4 21.7 %copy-start.10 = (u32[32]{0:T(128)S(1)}, u32[32]{0:T(128)}, u32[]{:S(2)}) copy-start(u32[32]{0:T(128)} %constant.204) | copy-start | bytes 388
  74.2 55.2 %copy-start.5 = (f32[1024]{0:T(1024)S(1)}, f32[1024]{0:T(1024)}, u32[]{:S(2)}) copy-start(f32[1024]{0:T(1024)} %param.25) | copy-start | bytes 12292
  74.2 55.2 %copy-start.6 = (f32[1024]{0:T(1024)S(1)}, f32[1024]{0:T(1024)}, u32[]{:S(2)}) copy-start(f32[1024]{0:T(1024)} %param.24) | copy-start | bytes 12292
  74.2 55.2 %copy-start.7 = (f32[1024]{0:T(1024)S(1)}, f32[1024]{0:T(1024)}, u32[]{:S(2)}) copy-start(f32[1024]{0:T(1024)} %param.26) | copy-start | bytes 12292
  74.2 483.0 %all-gather.12.cloned.1.call-start = ((), (), s32[]{:S(2)}) async-start(), calls=%async_computation.4 | async-start | bytes 83886080 | tf_op jit(solution)/shard_map/all_gather | solution.py:148
  76.8 45.5 %all-to-all-start.2 = ((bf16[8,56,1024]{2,1,0:T(8,128)(2,1)}), bf16[8,56,1024]{2,1,0:T(8,128)(2,1)S(1)}, u32[]{:S(2)}, u32[]{:S(2)}) async-start(bf16[8,56,1024]{2,1,0:T(8,128)(2,1)} %reshape.202), calls=%async_computation.2 | async-start | bytes 1835008 | tf_op jit(solution)/shard_map/all_to_all | solution.py:117
  601.7 93.3 %copy-start.8 = (f32[256]{0:T(256)S(1)}, f32[256]{0:T(256)}, u32[]{:S(2)}) copy-start(f32[256]{0:T(256)} %param.27) | copy-start | bytes 3076
  694.9 1.1 copy-start.9
Sparse Core Ops, SparseCore 0:
  74.3 90.2 all-gather.9
  166.2 390.9 all-gather.11
where the time goes:
time: 703 us
  waiting for transfers between devices  454 us (65%)
  blocking collectives  101 us (14%)
  local copies, waits for them, and re-layouts  62 us (9%)
  matrix products  45.4 us (6%)
  between operations  15.1 us (2%)
  starting transfers between devices  13.3 us (2%)
  other arithmetic  11.7 us (2%)
    all_gather x1, waiting for transfers between devices, body(): lax.all_gather(head_weight, 'mp', axis=0, tiled=True)  393 us
    all_gather x3, blocking collectives, combined_all(): gathered = jax.tree.map(lambda a: lax.all_gather(a, axis), part)  78.2 us
    dot_general x1, matrix products, body(): jnp.dot(block_rows, lax.all_gather(head_weight, 'mp', axis=0, tiled=True)...  44.4 us
    all_gather x1, waiting for transfers between devices, body(): lax.all_gather(own_rows, 'dp', axis=0, tiled=True)  34.8 us
    all_to_all x1, waiting for transfers between devices, body(): lax.all_to_all(reward_send, 'dp', split_axis=0, concat_axis=0, tiled=True)  25.9 us
  transfers between devices with their start and end apart: 4, of which 3 were waited for; matrix products, arithmetic and copies ran while one was open for 7% of the time, Pallas kernels for 0%

commit v1 on v0

v1 whole, which is shorter than its diff:
```python
import functools

import jax
import jax.numpy as jnp
from jax import lax
from jax.experimental import pallas as pl
from jax.experimental.pallas import tpu as pltpu
from jax.sharding import PartitionSpec as P

kl_coef = 0.1
discount = 0.99
gae_mix = 0.95
norm_eps = 1e-05


def xor_order(a, axis, me):
    size = a.shape[axis]
    bit = 1
    while bit < size:
        shape = a.shape
        split = shape[:axis] + (size // (2 * bit), 2, bit) + shape[axis + 1 :]
        b = a.reshape(split)
        a = jnp.where((me & bit) != 0, jnp.flip(b, axis + 1), b).reshape(shape)
        bit *= 2
    return a


def send_xor(a, axis, k):
    size = lax.axis_size(axis)
    return lax.ppermute(a, axis, [(i, i ^ k) for i in range(size)])


def x_size(shards):
    x = 1
    while 2 * x * 2 * x <= shards:
        x *= 2
    return x


def score_kernel(terms, part_ref, target_ref, *refs):
    rows = refs[:terms]
    weights = refs[terms : 2 * terms]
    out_ref = refs[2 * terms]
    logits = part_ref[...]
    for a, w in zip(rows, weights):
        logits += jnp.dot(a[0], w[...], preferred_element_type=jnp.float32)
    count, vocab = logits.shape
    row_max = jnp.max(logits, axis=1, keepdims=True)
    exp_total = jnp.sum(jnp.exp(logits - row_max), axis=1, keepdims=True)
    column = lax.broadcasted_iota(jnp.int32, (count, vocab), 1)
    target = jnp.sum(jnp.where(column == target_ref[...], logits, 0.0), axis=1, keepdims=True)
    lane = lax.broadcasted_iota(jnp.int32, (count, 128), 1)
    packed = jnp.where(lane == 0, row_max, jnp.where(lane == 1, exp_total, target))
    out_ref[...] = packed.T[:8]


def score_rows(part, target, rows, weights):
    tokens, vocab = part.shape
    block = 256
    width = weights[0].shape[0]
    terms = len(rows)
    in_specs = [
        pl.BlockSpec((block, vocab), lambda i: (i, 0)),
        pl.BlockSpec((block, 1), lambda i: (i, 0)),
    ]
    for _, m in rows:
        in_specs.append(
            pl.BlockSpec((1, block, width), functools.partial(lambda m, i: (m, i, 0), m))
        )
    in_specs += [pl.BlockSpec((width, vocab), lambda i: (0, 0))] * terms
    return pl.pallas_call(
        functools.partial(score_kernel, terms),
        grid=(tokens // block,),
        in_specs=in_specs,
        out_specs=pl.BlockSpec((8, block), lambda i: (0, i)),
        out_shape=jax.ShapeDtypeStruct((8, tokens), jnp.float32),
        compiler_params=pltpu.CompilerParams(vmem_limit_bytes=50 * 1024 * 1024),
        cost_estimate=pl.CostEstimate(
            flops=2 * tokens * vocab * width * terms,
            bytes_accessed=tokens * vocab * 4 + terms * width * (tokens + vocab) * 2,
            transcendentals=tokens * vocab,
        ),
    )(part, target, *[a for a, _ in rows], *weights)


def combine_stats(stats):
    top = jnp.max(stats[:, 0], axis=0)
    total = jnp.sum(stats[:, 1] * jnp.exp(stats[:, 0] - top[None]), axis=0)
    return jnp.stack([top, total, jnp.sum(stats[:, 2], axis=0)])


def body(
    token_ids,
    lengths,
    pack_dest,
    ref_hidden,
    reward_hidden,
    head_weight,
    norm_gain,
    score_weight,
    value_weight,
    old_logprob,
):
    shards = lax.axis_size("dp")
    ways = lax.axis_size("mp")
    me = lax.axis_index("dp")
    part_index = lax.axis_index("mp")
    req_dev, max_len, width = ref_hidden.shape
    slots = req_dev // 2 * (max_len + 1)
    per_pair = req_dev // shards
    run = slots // shards
    tokens = shards * slots
    x_ways = x_size(shards)
    z_ways = shards // x_ways
    vocab_row = head_weight.shape[1]
    vocab = vocab_row // ways

    weight_parts = []
    for k in range(ways):
        own = lax.dynamic_slice(
            head_weight, (0, (part_index ^ k) * vocab), (width, vocab)
        )
        weight_parts.append(own if k == 0 else send_xor(own, "mp", k))

    dest = xor_order(pack_dest.reshape(shards, req_dev), 0, me)
    lens = xor_order(lengths.reshape(shards, req_dev), 0, me)
    ids = xor_order(token_ids.reshape(shards, req_dev * max_len), 0, me)
    index = jnp.arange(req_dev, dtype=jnp.int32)
    order = dest * req_dev + index[None]
    before = order[:, None, :] < order[:, :, None]
    offsets = jnp.sum(jnp.where(before, lens[:, None, :], 0), axis=2)
    inner = jnp.arange(max_len, dtype=jnp.int32)
    valid = inner < lens[:, :, None]
    place = jnp.where(valid, offsets[:, :, None] + inner, -1).reshape(shards, -1)
    last = (inner == lens[:, :, None] - 1).reshape(shards, -1)
    slot_ids = jnp.arange(slots, dtype=jnp.int32)
    chosen = place[:, None, :] == slot_ids[None, :, None]
    target_last = jnp.sum(
        jnp.where(chosen, (2 * ids + last.astype(jnp.int32))[:, None, :], 0), axis=2
    )
    targets = target_last >> 1
    is_last = target_last & 1

    own_chosen = chosen[0]
    rows = jnp.dot(
        own_chosen.astype(jnp.bfloat16),
        ref_hidden.reshape(req_dev * max_len, width),
        preferred_element_type=jnp.float32,
    ).astype(jnp.bfloat16)
    held = jnp.stack([rows] + [send_xor(rows, "mp", 2 * m) for m in range(1, ways // 2)])
    pieces = []
    for z in range(z_ways):
        got = held if z == 0 else send_xor(held, "dp", z * x_ways)
        for x in range(x_ways):
            pieces.append(got if x == 0 else send_xor(got, "dp", x))
    even = jnp.stack(pieces, axis=1).reshape(ways // 2, tokens, width)
    odd = send_xor(even, "mp", 1)

    hidden = reward_hidden.reshape(req_dev * max_len, width).astype(jnp.float32)
    sums = jnp.stack(
        [
            jnp.sum(hidden * hidden, axis=1),
            jnp.sum(hidden * (norm_gain * score_weight), axis=1),
            jnp.sum(hidden * (norm_gain * value_weight), axis=1),
        ]
    )
    sums = jnp.sum(jnp.where(own_chosen[None], sums[:, None, :], 0.0), axis=2)
    sums = lax.psum(sums, "mp")
    sums = lax.all_to_all(
        jnp.transpose(sums.reshape(3, shards, run), (1, 0, 2)), "dp", 0, 0, tiled=True
    )
    sums = jnp.transpose(sums, (1, 0, 2)).reshape(3, slots)
    inv_rms = lax.rsqrt(sums[0] / (width * ways) + norm_eps)
    score = sums[1] * inv_rms
    value_est = sums[2] * inv_rms
    my_last = lax.dynamic_slice(
        xor_order(is_last, 0, me), (0, me * run), (shards, run)
    ).reshape(slots)
    not_last = 1.0 - my_last.astype(jnp.float32)
    next_value = jnp.concatenate([value_est[1:], jnp.zeros((1,), jnp.float32)])
    fixed = (
        jnp.where(my_last != 0, score, 0.0)
        + discount * next_value * not_last
        - value_est
        - kl_coef * old_logprob
    )

    part = jnp.dot(even[0], weight_parts[0], preferred_element_type=jnp.float32)
    part += jnp.dot(odd[0], weight_parts[1], preferred_element_type=jnp.float32)
    base = me * vocab_row + part_index * vocab
    stats = score_rows(
        part,
        (targets - base).reshape(tokens, 1),
        [(a, m) for m in range(1, ways // 2) for a in (even, odd)],
        weight_parts[2:],
    )[:3]

    stats = xor_order(stats.reshape(3, shards, shards, run), 1, me)
    stats = lax.all_to_all(jnp.transpose(stats, (2, 0, 1, 3)), "dp", 0, 0, tiled=True)
    stats = combine_stats(stats.reshape(shards, 3, slots))
    stats = combine_stats(lax.all_gather(stats, "mp"))
    ref_logprob = stats[2] - stats[0] - jnp.log(stats[1])

    td_error = fixed + kl_coef * ref_logprob
    decay = discount * gae_mix * not_last
    advantage = td_error
    for _ in range(max_len - 1):
        following = jnp.concatenate([advantage[1:], jnp.zeros((1,), jnp.float32)])
        advantage = td_error + decay * following
    return (ref_logprob, advantage)


def solution(mesh):
    return jax.shard_map(
        body,
        mesh=mesh,
        in_specs=(
            P(),
            P(),
            P(),
            P("dp", None, "mp"),
            P("dp", None, "mp"),
            P("mp", "dp"),
            P("mp"),
            P("mp"),
            P("mp"),
            P("dp"),
        ),
        out_specs=(P("dp"), P("dp")),
        check_vma=False,
    )
```

time: 703 us -> 410 us (0.58)
  waiting for transfers between devices: 454 us -> 258 us
  blocking collectives: 101 us -> 20.1 us
  Pallas kernels: 0 us -> 27.4 us
  local copies, waits for them, and re-layouts: 62 us -> 36.2 us
  between operations: 15.1 us -> 1.12 us
  starting transfers between devices: 13.3 us -> 26.7 us
  matrix products: 45.4 us -> 33.9 us
    all_gather x2 -> x0, waiting for transfers between devices: 427 us -> none  [the longest x1 393 us: body(): lax.all_gather(head_weight, 'mp', axis=0, tiled=True)]
    ppermute x0 -> x12, waiting for transfers between devices: none -> 251 us  [send_xor(): return lax.ppermute(a, axis, [(i, i ^ k) for i in range(size)])]
    all_gather x4 -> x1, blocking collectives: 84.1 us -> 5.63 us  [body(): stats = combine_stats(lax.all_gather(stats, 'mp'))]
    gather x13 -> x0, local copies, waits for them, and re-layouts: 51.8 us -> none  [the longest x1 11.8 us: body(): token_ids.reshape(-1)[(source_prompt * max_len + offset_in).reshape(-1)]]
    pallas_call x0 -> x1, Pallas kernels: none -> 27.4 us  [score_rows(): pl.pallas_call(functools.partial(score_kernel, terms), grid=(tokens // bl...]
    all_to_all x2, waiting for transfers between devices: 25.9 us -> 6.36 us  [the longest x1 6.36 us: body(): lax.all_to_all(jnp.transpose(stats, (2, 0, 1, 3)), 'dp', 0, 0, tiled=True)]
    ppermute x0 -> x12, starting transfers between devices: none -> 13.7 us  [send_xor(): return lax.ppermute(a, axis, [(i, i ^ k) for i in range(size)])]
    dot_general x2 -> x3, matrix products: 45.4 us -> 33.9 us  [the longest x1 18.3 us: body(): part = jnp.dot(even[0], weight_parts[0], preferred_element_type=jnp.float32)]
  transfers between devices with their start and end apart: 4 -> 14, of which waited for: 3 -> 8; matrix products, arithmetic and copies ran while one was open for 7% -> 14% of each run, Pallas kernels for 0% -> 7%
where the time goes in v1:
time: 410 us
  waiting for transfers between devices  258 us (63%)
  local copies, waits for them, and re-layouts  36.2 us (9%)
  matrix products  33.9 us (8%)
  Pallas kernels  27.4 us (7%)
  starting transfers between devices  26.7 us (7%)
  blocking collectives  20.1 us (5%)
  other arithmetic  7.01 us (2%)
    ppermute x12, waiting for transfers between devices, send_xor(): return lax.ppermute(a, axis, [(i, i ^ k) for i in range(size)])  251 us
    pallas_call x1, Pallas kernels, score_rows(): pl.pallas_call(functools.partial(score_kernel, terms), grid=(tokens // bl...  27.4 us
    dot_general x1, matrix products, body(): part = jnp.dot(even[0], weight_parts[0], preferred_element_type=jnp.float32)  18.3 us
    dot_general x1, matrix products, body(): part += jnp.dot(odd[0], weight_parts[1], preferred_element_type=jnp.float32)  15.1 us
    psum x1, blocking collectives, body(): sums = lax.psum(sums, 'mp')  14.4 us
    ppermute x12, starting transfers between devices, send_xor(): return lax.ppermute(a, axis, [(i, i ^ k) for i in range(size)])  13.7 us
    another operation x2, local copies, waits for them, and re-layouts, body(): even = jnp.stack(pieces, axis=1).reshape(ways // 2, tokens, width)  8.99 us
    dynamic_slice x1, local copies, waits for them, and re-layouts, body(): lax.dynamic_slice(head_weight, (0, (part_index ^ k) * vocab), (width, voc...  8.97 us
  transfers between devices with their start and end apart: 14, of which 8 were waited for; matrix products, arithmetic and copies ran while one was open for 14% of the time, Pallas kernels for 7%

profile of v1, /device:TPU:0, one launch (start us, length us, event | category | flops | bytes accessed | tf_op | source)
XLA Modules:
  0.0 409.9 jit_solution(11266128929551806083)
XLA Ops:
  7.1 3.0 collective-permute-start
  10.2 11.9 %collective-permute-done = bf16[256,1024]{1,0:T(8,128)(2,1)S(1)} collective-permute-done((bf16[256,1024]{1,0:T(8,128)(2,1)S(1)}, bf16[256,1024]{1,0:T(8,128)(2,1)S(1)}, u32[]{:S(2)}, u32[]{:S(2)}) %collective-permute-start) | collective-permute-done | bytes 524320 | tf_op jit(solution)/shard_map/ppermute | solution.py:30
  22.2 1.9 collective-permute-start.2
  24.0 2.6 collective-permute-start.4
  26.6 1.7 collective-permute-start.1
  28.4 39.5 %collective-permute-done.2 = bf16[2,256,1024]{2,1,0:T(8,128)(2,1)S(1)} collective-permute-done((bf16[2,256,1024]{2,1,0:T(8,128)(2,1)S(1)}, bf16[2,256,1024]{2,1,0:T(8,128)(2,1)S(1)}, u32[]{:S(2)}, u32[]{:S(2)}) %collective-permute-start.2) | collective-permute-done | bytes 1048608 | tf_op jit(solution)/shard_map/ppermute | solution.py:30
  67.9 1.4 collective-permute-start.3
  69.2 1.1 bitcast_dynamic-update-slice_fusion.7
  70.3 25.7 %collective-permute-done.4 = bf16[2,256,1024]{2,1,0:T(8,128)(2,1)S(1)} collective-permute-done((bf16[2,256,1024]{2,1,0:T(8,128)(2,1)S(1)}, bf16[2,256,1024]{2,1,0:T(8,128)(2,1)S(1)}, u32[]{:S(2)}, u32[]{:S(2)}) %collective-permute-start.4) | collective-permute-done | bytes 1048608 | tf_op jit(solution)/shard_map/ppermute | solution.py:30
  96.0 1.5 collective-permute-start.5
  98.0 1.1 bitcast_dynamic-update-slice_fusion.6
  99.1 1.1 bitcast_dynamic-update-slice_fusion.5
  100.2 1.1 bitcast_dynamic-update-slice_fusion.4
  101.2 1.0 bitcast_dynamic-update-slice_fusion.3
  102.3 19.8 %collective-permute-done.5 = bf16[2,256,1024]{2,1,0:T(8,128)(2,1)S(1)} collective-permute-done((bf16[2,256,1024]{2,1,0:T(8,128)(2,1)S(1)}, bf16[2,256,1024]{2,1,0:T(8,128)(2,1)S(1)}, u32[]{:S(2)}, u32[]{:S(2)}) %collective-permute-start.5) | collective-permute-done | bytes 1048608 | tf_op jit(solution)/shard_map/ppermute | solution.py:30
  122.1 1.1 bitcast_dynamic-update-slice_fusion.2
  123.2 1.1 bitcast_dynamic-update-slice_fusion.1
  124.2 12.0 %collective-permute-done.7 = bf16[2,256,1024]{2,1,0:T(8,128)(2,1)S(1)} collective-permute-done((bf16[2,256,1024]{2,1,0:T(8,128)(2,1)S(1)}, bf16[2,256,1024]{2,1,0:T(8,128)(2,1)S(1)}, u32[]{:S(2)}, u32[]{:S(2)}) %collective-permute-start.7) | collective-permute-done | bytes 1048608 | tf_op jit(solution)/shard_map/ppermute | solution.py:30
  137.3 7.9 %copy.43 = bf16[2,8,256,1024]{3,2,1,0:T(8,128)(2,1)} copy(bf16[2,8,256,1024]{3,2,0,1:T(8,128)(2,1)} %bitcast_dynamic-update-slice_fusion) | data formatting | bytes 16777216 | tf_op jit(solution)/shard_map/stack | solution.py:156
  145.2 9.0 %constant_dynamic-slice_fusion = (bf16[1024,2048]{1,0:T(8,128)(2,1)}, bf16[1024,2048]{1,0:T(8,128)(2,1)}, bf16[1024,2048]{1,0:T(8,128)(2,1)}) fusion(bf16[1024,8192]{1,0:T(8,128)(2,1)} %param.15, s32[]{:T(128)S(6)} %select_n.171, s32[]{:T(128)S(6)} %select_n.162, s32[]{:T(128)S(6)} %select_n.170), kind=kLoop, calls=%fused_computation.78 | loop fusion | bytes 25165836 | tf_op jit(solution)/shard_map/dynamic_slice | solution.py:120
  156.4 14.4 %psum.7 = f32[8,3,32]{2,0,1:T(8,128)S(1)} all-reduce(f32[8,3,32]{2,0,1:T(8,128)S(1)} %bitcast.109), channel_id=1, replica_groups=mesh['dp'=8,'mp'=4] {'mp'}, use_global_device_ids=true, to_apply=%region_12.13 | all-reduce | flops 768 | bytes 6144 | tf_op jit(solution)/shard_map/psum | solution.py:168
  171.4 7.0 %all-to-all-start.1 = ((f32[8,3,32]{2,1,0:T(4,128)}), f32[8,3,32]{2,1,0:T(4,128)S(1)}, u32[]{:S(2)}, u32[]{:S(2)}) async-start(f32[8,3,32]{2,1,0:T(4,128)} %copy.52), calls=%async_computation.1 | async-start | bytes 32768 | tf_op jit(solution)/shard_map/all_to_all | solution.py:169
  179.0 1.3 select_reduce_fusion
  181.3 2.7 slice.87
  184.0 15.1 %fusion = f32[2048,2048]{1,0:T(8,128)} fusion(bf16[1024,2048]{1,0:T(8,128)(2,1)} %collective-permute-done.9, bf16[2,2048,1024]{2,1,0:T(8,128)(2,1)} %collective-permute-done.8.refs_1_), kind=kOutput, calls=%fused_computation.2 | convolution fusion | flops 8589934592 | bytes 25165824 | tf_op jit(solution)/shard_map/dot_general | solution.py:189
  199.0 18.3 %convolution_add_fusion.part_ref = f32[2048,2048]{1,0:T(8,128)} fusion(f32[2048,2048]{1,0:T(8,128)} %fusion, bf16[2048,1024]{1,0:T(8,128)(2,1)S(1)} %bitcast.94, bf16[1024,8192]{1,0:T(8,128)(2,1)} %param.15, s32[]{:T(128)S(6)} %select_n.161), kind=kOutput, calls=%fused_computation | convolution fusion | flops 8594128896 | bytes 41943044 | tf_op jit(solution)/shard_map/dot_general | solution.py:188
  217.4 54.2 %collective-permute-done.11.refs_3_ = bf16[1024,2048]{1,0:T(8,128)(2,1)} collective-permute-done((bf16[1024,2048]{1,0:T(8,128)(2,1)}, bf16[1024,2048]{1,0:T(8,128)(2,1)}, u32[]{:S(2)}, u32[]{:S(2)}) %collective-permute-start.11) | collective-permute-done | bytes 4194336 | tf_op jit(solution)/shard_map/ppermute | solution.py:30
  271.6 88.0 %collective-permute-done.10.refs_2_ = bf16[1024,2048]{1,0:T(8,128)(2,1)} collective-permute-done((bf16[1024,2048]{1,0:T(8,128)(2,1)}, bf16[1024,2048]{1,0:T(8,128)(2,1)}, u32[]{:S(2)}, u32[]{:S(2)}) %collective-permute-start.10) | collective-permute-done | bytes 4194336 | tf_op jit(solution)/shard_map/ppermute | solution.py:30
  359.6 27.4 %shard_map.113 = f32[8,2048]{1,0:T(8,128)S(1)} custom-call(f32[2048,2048]{1,0:T(8,128)} %convolution_add_fusion.part_ref, s32[2048,1]{1,0:T(8,128)S(1)} %bitcast.91, bf16[2,2048,1024]{2,1,0:T(8,128)(2,1)} %bitcast.93, bf16[2,2048,1024]{2,1,0:T(8,128)(2,1)} %collective-permute-done.8.refs_1_, bf16[1024,2048]{1,0:T(8,128)(2,1)} %collective-permute-done.10.refs_2_, ...), custom_call_target="tpu_custom_call" | custom-call | flops 17179869184 | bytes 33554432 | tf_op jit(solution)/shard_map/pallas_call | solution.py:71
  388.0 6.0 %all-to-all-start = ((f32[8,1,768]{2,1,0:T(1,128)}), f32[8,1,768]{2,1,0:T(1,128)S(1)}, u32[]{:S(2)}, u32[]{:S(2)}) async-start(f32[8,1,768]{2,1,0:T(1,128)} %reshape.213), calls=%async_computation | async-start | bytes 49152 | tf_op jit(solution)/shard_map/all_to_all | solution.py:199
  394.2 6.4 %all-to-all-done = f32[8,1,768]{2,1,0:T(1,128)S(1)} async-done(((f32[8,1,768]{2,1,0:T(1,128)}), f32[8,1,768]{2,1,0:T(1,128)S(1)}, u32[]{:S(2)}, u32[]{:S(2)}) %all-to-all-start) | async-done | bytes 24608 | tf_op jit(solution)/shard_map/all_to_all | solution.py:199
  402.1 5.6 %all-gather.1 = f32[4,3,256]{2,1,0:T(4,128)S(1)} all-gather(f32[1,3,256]{2,1,0:T(4,128)S(1)} %maximum_bitcast_fusion), channel_id=2, replica_groups=mesh['dp'=8,'mp'=4] {'mp'}, dimensions={0}, use_global_device_ids=true | all-gather | bytes 15360 | tf_op jit(solution)/shard_map/all_gather | solution.py:201
  (119 shorter events, 16.9 us)
Async XLA Ops:
  0.6 5.2 %copy-start.1 = (bf16[64,7,1024]{2,0,1:T(8,128)(2,1)S(1)}, bf16[64,7,1024]{2,0,1:T(8,128)(2,1)}, u32[]{:S(2)}) copy-start(bf16[64,7,1024]{2,0,1:T(8,128)(2,1)} %param.13) | copy-start | bytes 2752516
  7.1 15.0 %collective-permute-start = (bf16[256,1024]{1,0:T(8,128)(2,1)S(1)}, bf16[256,1024]{1,0:T(8,128)(2,1)S(1)}, u32[]{:S(2)}, u32[]{:S(2)}) collective-permute-start(bf16[256,1024]{1,0:T(8,128)(2,1)S(1)} %convolution_convert_fusion), channel_id=1, source_target_pairs={{0,2},{1,3},{2,0},{3,1},{4,6},{5,7},{6,4},{7,5},{8,10},{9,11},{10,... | collective-permute-start | bytes 1572872 | tf_op jit(solution)/shard_map/ppermute | solution.py:30
  22.2 45.7 %collective-permute-start.2 = (bf16[2,256,1024]{2,1,0:T(8,128)(2,1)S(1)}, bf16[2,256,1024]{2,1,0:T(8,128)(2,1)S(1)}, u32[]{:S(2)}, u32[]{:S(2)}) collective-permute-start(bf16[2,256,1024]{2,1,0:T(8,128)(2,1)S(1)} %pad_maximum_fusion), channel_id=1, source_target_pairs={{0,8},{4,12},{8,0},{12,4},{16,24},{20,28},{24,16},{28,20},{1,9},{5... | collective-permute-start | bytes 3145736 | tf_op jit(solution)/shard_map/ppermute | solution.py:30
  24.0 71.9 %collective-permute-start.4 = (bf16[2,256,1024]{2,1,0:T(8,128)(2,1)S(1)}, bf16[2,256,1024]{2,1,0:T(8,128)(2,1)S(1)}, u32[]{:S(2)}, u32[]{:S(2)}) collective-permute-start(bf16[2,256,1024]{2,1,0:T(8,128)(2,1)S(1)} %pad_maximum_fusion), channel_id=1, source_target_pairs={{0,16},{4,20},{8,24},{12,28},{16,0},{20,4},{24,8},{28,12},{1,17},{... | collective-permute-start | bytes 3145736 | tf_op jit(solution)/shard_map/ppermute | solution.py:30
  26.6 70.8 %collective-permute-start.6 = (bf16[2,256,1024]{2,1,0:T(8,128)(2,1)S(1)}, bf16[2,256,1024]{2,1,0:T(8,128)(2,1)S(1)}, u32[]{:S(2)}, u32[]{:S(2)}) collective-permute-start(bf16[2,256,1024]{2,1,0:T(8,128)(2,1)S(1)} %pad_maximum_fusion), channel_id=1, source_target_pairs={{0,24},{4,28},{8,16},{12,20},{16,8},{20,12},{24,0},{28,4},{1,25},{... | collective-permute-start | bytes 3145736 | tf_op jit(solution)/shard_map/ppermute | solution.py:30
  26.6 71.4 %collective-permute-start.1 = (bf16[2,256,1024]{2,1,0:T(8,128)(2,1)S(1)}, bf16[2,256,1024]{2,1,0:T(8,128)(2,1)S(1)}, u32[]{:S(2)}, u32[]{:S(2)}) collective-permute-start(bf16[2,256,1024]{2,1,0:T(8,128)(2,1)S(1)} %pad_maximum_fusion), channel_id=1, source_target_pairs={{0,4},{4,0},{8,12},{12,8},{16,20},{20,16},{24,28},{28,24},{1,5},{5... | collective-permute-start | bytes 3145736 | tf_op jit(solution)/shard_map/ppermute | solution.py:30
  67.9 32.3 %collective-permute-start.3 = (bf16[2,256,1024]{2,1,0:T(8,128)(2,1)S(1)}, bf16[2,256,1024]{2,1,0:T(8,128)(2,1)S(1)}, u32[]{:S(2)}, u32[]{:S(2)}) collective-permute-start(bf16[2,256,1024]{2,1,0:T(8,128)(2,1)S(1)} %collective-permute-done.2), channel_id=1, source_target_pairs={{0,4},{4,0},{8,12},{12,8},{16,20},{20,16},{24,28},{28,24},{1,5},{5... | collective-permute-start | bytes 3145736 | tf_op jit(solution)/shard_map/ppermute | solution.py:30
  96.0 26.1 %collective-permute-start.5 = (bf16[2,256,1024]{2,1,0:T(8,128)(2,1)S(1)}, bf16[2,256,1024]{2,1,0:T(8,128)(2,1)S(1)}, u32[]{:S(2)}, u32[]{:S(2)}) collective-permute-start(bf16[2,256,1024]{2,1,0:T(8,128)(2,1)S(1)} %collective-permute-done.4), channel_id=1, source_target_pairs={{0,4},{4,0},{8,12},{12,8},{16,20},{20,16},{24,28},{28,24},{1,5},{5... | collective-permute-start | bytes 3145736 | tf_op jit(solution)/shard_map/ppermute | solution.py:30
  97.5 38.7 %collective-permute-start.7 = (bf16[2,256,1024]{2,1,0:T(8,128)(2,1)S(1)}, bf16[2,256,1024]{2,1,0:T(8,128)(2,1)S(1)}, u32[]{:S(2)}, u32[]{:S(2)}) collective-permute-start(bf16[2,256,1024]{2,1,0:T(8,128)(2,1)S(1)} %collective-permute-done.6), channel_id=1, source_target_pairs={{0,4},{4,0},{8,12},{12,8},{16,20},{20,16},{24,28},{28,24},{1,5},{5... | collective-permute-start | bytes 3145736 | tf_op jit(solution)/shard_map/ppermute | solution.py:30
  145.2 38.8 %collective-permute-start.8 = (bf16[2,2048,1024]{2,1,0:T(8,128)(2,1)}, bf16[2,2048,1024]{2,1,0:T(8,128)(2,1)}, u32[]{:S(2)}, u32[]{:S(2)}) collective-permute-start(bf16[2,2048,1024]{2,1,0:T(8,128)(2,1)} %bitcast.92), channel_id=1, source_target_pairs={{0,1},{1,0},{2,3},{3,2},{4,5},{5,4},{6,7},{7,6},{8,9},{9,8},{10,11... | collective-permute-start | bytes 25165832 | tf_op jit(solution)/shard_map/ppermute | solution.py:30
  145.2 9.5 %copy-start.2 = (f32[1024]{0:T(1024)S(1)}, f32[1024]{0:T(1024)}, u32[]{:S(2)}) copy-start(f32[1024]{0:T(1024)} %param.16) | copy-start | bytes 12292
  145.2 9.5 %copy-start.3 = (f32[1024]{0:T(1024)S(1)}, f32[1024]{0:T(1024)}, u32[]{:S(2)}) copy-start(f32[1024]{0:T(1024)} %param.18) | copy-start | bytes 12292
  145.2 9.5 %copy-start.4 = (f32[1024]{0:T(1024)S(1)}, f32[1024]{0:T(1024)}, u32[]{:S(2)}) copy-start(f32[1024]{0:T(1024)} %param.17) | copy-start | bytes 12292
  145.2 9.5 %copy-start = (bf16[64,7,1024]{2,0,1:T(8,128)(2,1)S(1)}, bf16[64,7,1024]{2,0,1:T(8,128)(2,1)}, u32[]{:S(2)}) copy-start(bf16[64,7,1024]{2,0,1:T(8,128)(2,1)} %param.14) | copy-start | bytes 2752516
  154.2 29.7 %collective-permute-start.9 = (bf16[1024,2048]{1,0:T(8,128)(2,1)}, bf16[1024,2048]{1,0:T(8,128)(2,1)}, u32[]{:S(2)}, u32[]{:S(2)}) collective-permute-start(bf16[1024,2048]{1,0:T(8,128)(2,1)} %get-tuple-element.14), channel_id=1, source_target_pairs={{0,1},{1,0},{2,3},{3,2},{4,5},{5,4},{6,7},{7,6},{8,9},{9,8},{10,11... | collective-permute-start | bytes 12582920 | tf_op jit(solution)/shard_map/ppermute | solution.py:30
  171.4 216.5 %all-to-all-start.1 = ((f32[8,3,32]{2,1,0:T(4,128)}), f32[8,3,32]{2,1,0:T(4,128)S(1)}, u32[]{:S(2)}, u32[]{:S(2)}) async-start(f32[8,3,32]{2,1,0:T(4,128)} %copy.52), calls=%async_computation.1 | async-start | bytes 32768 | tf_op jit(solution)/shard_map/all_to_all | solution.py:169
  178.4 93.2 %collective-permute-start.11 = (bf16[1024,2048]{1,0:T(8,128)(2,1)}, bf16[1024,2048]{1,0:T(8,128)(2,1)}, u32[]{:S(2)}, u32[]{:S(2)}) collective-permute-start(bf16[1024,2048]{1,0:T(8,128)(2,1)} %get-tuple-element.13), channel_id=1, source_target_pairs={{0,3},{1,2},{2,1},{3,0},{4,7},{5,6},{6,5},{7,4},{8,11},{9,10},{10,... | collective-permute-start | bytes 12582920 | tf_op jit(solution)/shard_map/ppermute | solution.py:30
  178.5 181.2 %collective-permute-start.10 = (bf16[1024,2048]{1,0:T(8,128)(2,1)}, bf16[1024,2048]{1,0:T(8,128)(2,1)}, u32[]{:S(2)}, u32[]{:S(2)}) collective-permute-start(bf16[1024,2048]{1,0:T(8,128)(2,1)} %get-tuple-element.15), channel_id=1, source_target_pairs={{0,2},{1,3},{2,0},{3,1},{4,6},{5,7},{6,4},{7,5},{8,10},{9,11},{10,... | collective-permute-start | bytes 12582920 | tf_op jit(solution)/shard_map/ppermute | solution.py:30
  359.6 48.1 %copy-start.5 = (f32[256]{0:T(256)S(1)}, f32[256]{0:T(256)}, u32[]{:S(2)}) copy-start(f32[256]{0:T(256)} %param.19) | copy-start | bytes 3076
  388.0 12.6 %all-to-all-start = ((f32[8,1,768]{2,1,0:T(1,128)}), f32[8,1,768]{2,1,0:T(1,128)S(1)}, u32[]{:S(2)}, u32[]{:S(2)}) async-start(f32[8,1,768]{2,1,0:T(1,128)} %reshape.213), calls=%async_computation | async-start | bytes 49152 | tf_op jit(solution)/shard_map/all_to_all | solution.py:199

commit v2 on v1

--- a/solution.py
+++ b/solution.py
@@ -25,9 +25,13 @@
     return a
 
 
-def send_xor(a, axis, k):
-    size = lax.axis_size(axis)
-    return lax.ppermute(a, axis, [(i, i ^ k) for i in range(size)])
+def flip(a, k):
+    bit = 1
+    while bit <= k:
+        if k & bit:
+            a = a + bit - 2 * bit * ((a // bit) % 2)
+        bit *= 2
+    return a
 
 
 def x_size(shards):
@@ -35,6 +39,152 @@
     while 2 * x * 2 * x <= shards:
         x *= 2
     return x
+
+
+def exchange_kernel(
+    shards, ways, rows_ref, weight_ref, held, got, part, w_scratch,
+    y_sems, z_sems, x_sems, c_sems, w_sems, local_sems,
+):
+    me = lax.axis_index("dp")
+    place = lax.axis_index("mp")
+    x_ways = x_size(shards)
+    z_ways = shards // x_ways
+    halves = ways // 2
+    slots, width = rows_ref.shape
+    tokens = held.shape[1]
+    vocab = got.shape[2]
+
+    peers = [{"mp": flip(place, k)} for k in range(1, ways)]
+    peers += [{"dp": flip(me, z * x_ways)} for z in range(1, z_ways)]
+    peers += [{"dp": flip(me, x)} for x in range(1, x_ways)]
+    barrier = pltpu.get_barrier_semaphore()
+    for peer in peers:
+        pl.semaphore_signal(
+            barrier, inc=1, device_id=peer, device_id_type=pl.DeviceIdType.MESH
+        )
+    pl.semaphore_wait(barrier, len(peers))
+
+    started = []
+
+    def send(src, dst, sems, i, peer):
+        copy = pltpu.make_async_remote_copy(
+            src_ref=src,
+            dst_ref=dst,
+            send_sem=sems.at[0, i],
+            recv_sem=sems.at[1, i],
+            device_id=peer,
+            device_id_type=pl.DeviceIdType.MESH,
+        )
+        copy.start()
+        started.append(copy)
+        return copy
+
+    def slot(k, r, count=1):
+        return held.at[k, pl.ds(r * slots, count * slots), :]
+
+    def columns(k):
+        return weight_ref.at[:, pl.ds(pl.multiple_of(flip(place, k) * vocab, vocab), vocab)]
+
+    own_rows = pltpu.make_async_copy(rows_ref, slot(0, 0), local_sems.at[0])
+    own_rows.start()
+    y_copy, z_copy, x_copy, c_copy, w_copy = {}, {}, {}, {}, {}
+    for m in range(1, halves):
+        y_copy[m] = send(rows_ref, slot(2 * m, 0), y_sems, m, {"mp": flip(place, 2 * m)})
+    for k in list(range(2, ways)) + [1]:
+        w_copy[k] = send(columns(k), got.at[k - 1], w_sems, k, {"mp": flip(place, k)})
+    own_weight = pltpu.make_async_copy(columns(0), w_scratch.at[0], local_sems.at[1])
+    own_weight.start()
+
+    def spread(m, z):
+        src = rows_ref if m == 0 and z == 0 else slot(2 * m, z * x_ways)
+        if z == 0:
+            for z_to in range(1, z_ways):
+                z_copy[m, z_to] = send(
+                    src, slot(2 * m, z_to * x_ways), z_sems, m * z_ways + z_to,
+                    {"dp": flip(me, z_to * x_ways)},
+                )
+        for x in range(1, x_ways):
+            x_copy[m, z, x] = send(
+                src, slot(2 * m, z * x_ways + x), x_sems, (m * z_ways + z) * x_ways + x,
+                {"dp": flip(me, x)},
+            )
+
+    spread(0, 0)
+    for m in range(1, halves):
+        y_copy[m].wait_recv()
+        spread(m, 0)
+    for z in range(1, z_ways):
+        for m in range(halves):
+            z_copy[m, z].wait_recv()
+            spread(m, z)
+    own_rows.wait()
+    for z in range(z_ways):
+        for m in range(halves):
+            for x in range(1, x_ways):
+                x_copy[m, z, x].wait_recv()
+            c_copy[m, z] = send(
+                slot(2 * m, z * x_ways, x_ways), slot(2 * m + 1, z * x_ways, x_ways),
+                c_sems, m * z_ways + z, {"mp": flip(place, 1)},
+            )
+    own_weight.wait()
+    w_copy[1].wait_recv()
+    next_weight = pltpu.make_async_copy(got.at[0], w_scratch.at[1], local_sems.at[2])
+    next_weight.start()
+    next_weight.wait()
+    for c in c_copy.values():
+        c.wait_recv()
+
+    def multiply(a_ref, b_ref, out_ref):
+        out_ref[...] = jnp.dot(
+            a_ref[...], w_scratch[0], preferred_element_type=jnp.float32
+        ) + jnp.dot(b_ref[...], w_scratch[1], preferred_element_type=jnp.float32)
+
+    block = 256
+    pltpu.emit_pipeline(
+        multiply,
+        grid=(tokens // block,),
+        in_specs=[pl.BlockSpec((block, width), lambda i: (i, 0))] * 2,
+        out_specs=[pl.BlockSpec((block, vocab), lambda i: (i, 0))],
+    )(held.at[0], held.at[1], part)
+    for k in range(2, ways):
+        w_copy[k].wait_recv()
+    for copy in started:
+        copy.wait_send()
+
+
+def exchange(rows, head_weight, shards, ways):
+    slots, width = rows.shape
+    tokens = shards * slots
+    vocab = head_weight.shape[1] // ways
+    halves = ways // 2
+    pairs = lambda count: pltpu.SemaphoreType.DMA((2, count))
+    return pl.pallas_call(
+        functools.partial(exchange_kernel, shards, ways),
+        in_specs=[pl.BlockSpec(memory_space=pl.ANY)] * 2,
+        out_specs=[pl.BlockSpec(memory_space=pl.ANY)] * 3,
+        out_shape=[
+            jax.ShapeDtypeStruct((ways, tokens, width), rows.dtype),
+            jax.ShapeDtypeStruct((ways - 1, width, vocab), head_weight.dtype),
+            jax.ShapeDtypeStruct((tokens, vocab), jnp.float32),
+        ],
+        scratch_shapes=[
+            pltpu.VMEM((2, width, vocab), head_weight.dtype),
+            pairs(halves),
+            pairs(halves * shards),
+            pairs(halves * shards),
+            pairs(halves * shards),
+            pairs(ways),
+            pltpu.SemaphoreType.DMA((3,)),
+        ],
+        compiler_params=pltpu.CompilerParams(
+            collective_id=0, has_side_effects=True, vmem_limit_bytes=48 * 1024 * 1024
+        ),
+        cost_estimate=pl.CostEstimate(
+            flops=4 * tokens * vocab * width,
+            bytes_accessed=2 * ways * width * (tokens + vocab) + 4 * tokens * vocab,
+            transcendentals=0,
+        ),
+    )(rows, head_weight)
 
 
 def score_kernel(terms, part_ref, target_ref, *refs):
@@ -43,7 +193,7 @@
     out_ref = refs[2 * terms]
     logits = part_ref[...]
     for a, w in zip(rows, weights):
-        logits += jnp.dot(a[0], w[...], preferred_element_type=jnp.float32)
+        logits += jnp.dot(a[0], w[0], preferred_element_type=jnp.float32)
     count, vocab = logits.shape
     row_max = jnp.max(logits, axis=1, keepdims=True)
     exp_total = jnp.sum(jnp.exp(logits - row_max), axis=1, keepdims=True)
@@ -54,20 +204,23 @@
     out_ref[...] = packed.T[:8]
 
 
-def score_rows(part, target, rows, weights):
+def score_rows(part, target, held, got):
     tokens, vocab = part.shape
     block = 256
-    width = weights[0].shape[0]
-    terms = len(rows)
+    ways, _, width = held.shape
+    terms = ways - 2
     in_specs = [
         pl.BlockSpec((block, vocab), lambda i: (i, 0)),
         pl.BlockSpec((block, 1), lambda i: (i, 0)),
     ]
-    for _, m in rows:
+    for k in range(2, ways):
         in_specs.append(
-            pl.BlockSpec((1, block, width), functools.partial(lambda m, i: (m, i, 0), m))
+            pl.BlockSpec((1, block, width), functools.partial(lambda k, i: (k, i, 0), k))
         )
-    in_specs += [pl.BlockSpec((width, vocab), lambda i: (0, 0))] * terms
+    for k in range(2, ways):
+        in_specs.append(
+            pl.BlockSpec((1, width, vocab), functools.partial(lambda k, i: (k - 1, 0, 0), k))
+        )
     return pl.pallas_call(
         functools.partial(score_kernel, terms),
         grid=(tokens // block,),
@@ -80,7 +233,7 @@
             bytes_accessed=tokens * vocab * 4 + terms * width * (tokens + vocab) * 2,
             transcendentals=tokens * vocab,
         ),
-    )(part, target, *[a for a, _ in rows], *weights)
+    )(part, target, *[held] * terms, *[got] * terms)
 
 
 def combine_stats(stats):
@@ -110,17 +263,8 @@
     per_pair = req_dev // shards
     run = slots // shards
     tokens = shards * slots
-    x_ways = x_size(shards)
-    z_ways = shards // x_ways
     vocab_row = head_weight.shape[1]
     vocab = vocab_row // ways
-
-    weight_parts = []
-    for k in range(ways):
-        own = lax.dynamic_slice(
-            head_weight, (0, (part_index ^ k) * vocab), (width, vocab)
-        )
-        weight_parts.append(own if k == 0 else send_xor(own, "mp", k))
 
     dest = xor_order(pack_dest.reshape(shards, req_dev), 0, me)
     lens = xor_order(lengths.reshape(shards, req_dev), 0, me)
@@ -147,14 +291,7 @@
         ref_hidden.reshape(req_dev * max_len, width),
         preferred_element_type=jnp.float32,
     ).astype(jnp.bfloat16)
-    held = jnp.stack([rows] + [send_xor(rows, "mp", 2 * m) for m in range(1, ways // 2)])
-    pieces = []
-    for z in range(z_ways):
-        got = held if z == 0 else send_xor(held, "dp", z * x_ways)
-        for x in range(x_ways):
-            pieces.append(got if x == 0 else send_xor(got, "dp", x))
-    even = jnp.stack(pieces, axis=1).reshape(ways // 2, tokens, width)
-    odd = send_xor(even, "mp", 1)
+    held, got, part = exchange(rows, head_weight, shards, ways)
 
     hidden = reward_hidden.reshape(req_dev * max_len, width).astype(jnp.float32)
     sums = jnp.stack(
@@ -165,43 +302,29 @@
         ]
     )
     sums = jnp.sum(jnp.where(own_chosen[None], sums[:, None, :], 0.0), axis=2)
-    sums = lax.psum(sums, "mp")
-    sums = lax.all_to_all(
-        jnp.transpose(sums.reshape(3, shards, run), (1, 0, 2)), "dp", 0, 0, tiled=True
-    )
-    sums = jnp.transpose(sums, (1, 0, 2)).reshape(3, slots)
-    inv_rms = lax.rsqrt(sums[0] / (width * ways) + norm_eps)
-    score = sums[1] * inv_rms
-    value_est = sums[2] * inv_rms
     my_last = lax.dynamic_slice(
         xor_order(is_last, 0, me), (0, me * run), (shards, run)
     ).reshape(slots)
     not_last = 1.0 - my_last.astype(jnp.float32)
+    base = me * vocab_row + part_index * vocab
+    stats = score_rows(part, (targets - base).reshape(tokens, 1), held, got)[:3]
+
+    stats = xor_order(stats.reshape(3, shards, shards, run), 1, me)
+    sent = jnp.concatenate([stats, sums.reshape(3, 1, shards, run)], axis=1)
+    taken = lax.all_to_all(jnp.transpose(sent, (2, 0, 1, 3)), "dp", 0, 0, tiled=True)
+    stats = combine_stats(taken[:, :, :shards].reshape(shards, 3, slots))
+    sums = jnp.transpose(taken[:, :, shards], (1, 0, 2)).reshape(3, slots)
+    gathered = lax.all_gather(jnp.concatenate([stats, sums]), "mp")
+    stats = combine_stats(gathered[:, :3])
+    sums = jnp.sum(gathered[:, 3:], axis=0)
+    ref_logprob = stats[2] - stats[0] - jnp.log(stats[1])
+
+    inv_rms = lax.rsqrt(sums[0] / (width * ways) + norm_eps)
+    score = sums[1] * inv_rms
+    value_est = sums[2] * inv_rms
     next_value = jnp.concatenate([value_est[1:], jnp.zeros((1,), jnp.float32)])
-    fixed = (
-        jnp.where(my_last != 0, score, 0.0)
-        + discount * next_value * not_last
-        - value_est
-        - kl_coef * old_logprob
-    )
-
-    part = jnp.dot(even[0], weight_parts[0], preferred_element_type=jnp.float32)
-    part += jnp.dot(odd[0], weight_parts[1], preferred_element_type=jnp.float32)
-    base = me * vocab_row + part_index * vocab
-    stats = score_rows(
-        part,
-        (targets - base).reshape(tokens, 1),
-        [(a, m) for m in range(1, ways // 2) for a in (even, odd)],
-        weight_parts[2:],
-    )[:3]
-
-    stats = xor_order(stats.reshape(3, shards, shards, run), 1, me)
-    stats = lax.all_to_all(jnp.transpose(stats, (2, 0, 1, 3)), "dp", 0, 0, tiled=True)
-    stats = combine_stats(stats.reshape(shards, 3, slots))
-    stats = combine_stats(lax.all_gather(stats, "mp"))
-    ref_logprob = stats[2] - stats[0] - jnp.log(stats[1])
-
-    td_error = fixed + kl_coef * ref_logprob
+    reward = -kl_coef * (old_logprob - ref_logprob) + jnp.where(my_last != 0, score, 0.0)
+    td_error = reward + discount * next_value * not_last - value_est
     decay = discount * gae_mix * not_last
     advantage = td_error
     for _ in range(max_len - 1):

time: 410 us -> 259 us (0.63)
  waiting for transfers between devices: 258 us -> 6.16 us
  Pallas kernels: 27.4 us -> 225 us
  matrix products: 33.9 us -> 0.49 us
  local copies, waits for them, and re-layouts: 36.2 us -> 8.47 us
  starting transfers between devices: 26.7 us -> 3.89 us
  blocking collectives: 20.1 us -> 5.19 us
    ppermute x12 -> x0, waiting for transfers between devices: 251 us -> none  [send_xor(): return lax.ppermute(a, axis, [(i, i ^ k) for i in range(size)])]
    pallas_call x0 -> x1, Pallas kernels: none -> 198 us  [exchange(): pl.pallas_call(functools.partial(exchange_kernel, shards, ways), in_specs...]
    dot_general x2 -> x0, matrix products: 33.4 us -> none  [the longest x1 18.3 us: body(): part = jnp.dot(even[0], weight_parts[0], preferred_element_type=jnp.float32)]
    psum x1 -> x0, blocking collectives: 14.4 us -> none  [body(): sums = lax.psum(sums, 'mp')]
    ppermute x12 -> x0, starting transfers between devices: 13.7 us -> none  [send_xor(): return lax.ppermute(a, axis, [(i, i ^ k) for i in range(size)])]
    all_to_all x2 -> x1, starting transfers between devices: 13 us -> 3.89 us  [body(): lax.all_to_all(jnp.transpose(sent, (2, 0, 1, 3)), 'dp', 0, 0, tiled=True)]
    another operation x3 -> x1, local copies, waits for them, and re-layouts: 9.09 us -> 0.1 us  [the longest x2 8.99 us: body(): even = jnp.stack(pieces, axis=1).reshape(ways // 2, tokens, width)]
    dynamic_slice x1 -> x0, local copies, waits for them, and re-layouts: 8.97 us -> none  [body(): lax.dynamic_slice(head_weight, (0, (part_index ^ k) * vocab), (width, voc...]
  transfers between devices with their start and end apart: 14 -> 1, of which waited for: 8 -> 1; matrix products, arithmetic and copies ran while one was open for 14% -> 0% of each run, Pallas kernels for 7% -> 0%
where the time goes in v2:
time: 259 us
  Pallas kernels  225 us (87%)
  local copies, waits for them, and re-layouts  8.47 us (3%)
  other arithmetic  7.88 us (3%)
  waiting for transfers between devices  6.16 us (2%)
  blocking collectives  5.19 us (2%)
  starting transfers between devices  3.89 us (2%)
    pallas_call x1, Pallas kernels, exchange(): pl.pallas_call(functools.partial(exchange_kernel, shards, ways), in_specs...  198 us
    pallas_call x1, Pallas kernels, score_rows(): pl.pallas_call(functools.partial(score_kernel, terms), grid=(tokens // bl...  27.4 us
    all_to_all x1, waiting for transfers between devices, body(): lax.all_to_all(jnp.transpose(sent, (2, 0, 1, 3)), 'dp', 0, 0, tiled=True)  6.16 us
    all_gather x1, blocking collectives, body(): gathered = lax.all_gather(jnp.concatenate([stats, sums]), 'mp')  5.19 us
  transfers between devices with their start and end apart: 1, of which 1 were waited for; matrix products, arithmetic and copies ran while one was open for 0% of the time, Pallas kernels for 0%

profile of v2, /device:TPU:0, one launch (start us, length us, event | category | flops | bytes accessed | tf_op | source)
XLA Modules:
  0.0 258.6 jit_solution(10042024620421384537)
XLA Ops:
  0.6 0.8 fusion.30
  1.4 1.7 fusion
  3.3 0.1 stack.23
  3.5 0.1 stack.22
  3.7 0.1 stack.21
  3.9 0.9 copy.40
  4.7 0.2 reshape_reshape.48
  4.9 0.2 rev.63
  5.2 0.8 reshape_reshape.45
  6.0 0.8 reshape_reshape.42
  7.0 0.2 eq.35
  7.2 0.1 lt.54
  7.3 0.3 select_reduce_fusion.2
  7.8 0.2 add.86
  8.1 0.2 lt.58
  8.3 0.7 iota_compare_fusion
  9.0 0.3 select_reduce_fusion.1
  9.4 0.5 copy.39
  9.9 0.3 reshape.182
  10.2 0.5 convolution_convert_fusion.rows_ref
  10.7 1.3 select_reduce_fusion
  12.1 0.4 copy.54
  12.4 198.1 %shard_map.113 = (bf16[4,2048,1024]{2,1,0:T(8,128)(2,1)}, bf16[3,1024,2048]{2,1,0:T(8,128)(2,1)}, f32[2048,2048]{1,0:T(8,128)}) custom-call(bf16[256,1024]{1,0:T(8,128)(2,1)S(1)} %convolution_convert_fusion.rows_ref, bf16[1024,8192]{1,0:T(8,128)(2,1)} %weight_ref.1), custom_call_target="tpu_custom_call" | custom-call | flops 17179869184 | bytes 50331648 | tf_op jit(solution)/shard_map/pallas_call | solution.py:161
  210.5 27.4 %shard_map.114 = f32[8,2048]{1,0:T(8,128)S(1)} custom-call(f32[2048,2048]{1,0:T(8,128)} %get-tuple-element.5.part_ref, s32[2048,1]{1,0:T(8,128)S(1)} %bitcast.76, bf16[4,2048,1024]{2,1,0:T(8,128)(2,1)} %get-tuple-element.6.refs_0_.refs_1_, bf16[4,2048,1024]{2,1,0:T(8,128)(2,1)} %get-tuple-element.6.refs_0_.refs_1_, ...), custom_call_target="tpu_custom_call" | custom-call | flops 17179869184 | bytes 33554432 | tf_op jit(solution)/shard_map/pallas_call | solution.py:224
  238.2 0.7 reshape.192
  239.0 3.9 %all-to-all-start = ((f32[8,1,864]{2,1,0:T(1,128)}), f32[8,1,864]{2,1,0:T(1,128)S(1)}, u32[]{:S(2)}, u32[]{:S(2)}) async-start(f32[8,1,864]{2,1,0:T(1,128)} %reshape.192), calls=%async_computation | async-start | bytes 57344 | tf_op jit(solution)/shard_map/all_to_all | solution.py:314
  243.4 6.2 %all-to-all-done = f32[8,1,864]{2,1,0:T(1,128)S(1)} async-done(((f32[8,1,864]{2,1,0:T(1,128)}), f32[8,1,864]{2,1,0:T(1,128)S(1)}, u32[]{:S(2)}, u32[]{:S(2)}) %all-to-all-start) | async-done | bytes 27680 | tf_op jit(solution)/shard_map/all_to_all | solution.py:314
  249.5 0.5 broadcast.114
  250.0 0.7 reduce.7
  251.2 5.2 %all-gather.1 = f32[4,6,256]{2,1,0:T(8,128)S(1)} all-gather(f32[1,6,256]{2,1,0:T(8,128)S(1)} %maximum_bitcast_fusion.1), channel_id=2, replica_groups=mesh['dp'=8,'mp'=4] {'mp'}, dimensions={0}, use_global_device_ids=true | all-gather | bytes 30720 | tf_op jit(solution)/shard_map/all_gather | solution.py:317
  256.6 0.6 fusion.15
  258.0 0.6 fusion.27
  (76 shorter events, 3.1 us)
Async XLA Ops:
  0.6 8.7 %copy-start = (bf16[64,7,1024]{2,0,1:T(8,128)(2,1)S(1)}, bf16[64,7,1024]{2,0,1:T(8,128)(2,1)}, u32[]{:S(2)}) copy-start(bf16[64,7,1024]{2,0,1:T(8,128)(2,1)} %param.13) | copy-start | bytes 2752516
  210.5 46.0 %copy-start.1 = (f32[256]{0:T(256)S(1)}, f32[256]{0:T(256)}, u32[]{:S(2)}) copy-start(f32[256]{0:T(256)} %param.19) | copy-start | bytes 3076
  239.0 10.6 %all-to-all-start = ((f32[8,1,864]{2,1,0:T(1,128)}), f32[8,1,864]{2,1,0:T(1,128)S(1)}, u32[]{:S(2)}, u32[]{:S(2)}) async-start(f32[8,1,864]{2,1,0:T(1,128)} %reshape.192), calls=%async_computation | async-start | bytes 57344 | tf_op jit(solution)/shard_map/all_to_all | solution.py:314

commit v3 on v2

--- a/solution.py
+++ b/solution.py
@@ -41,9 +41,21 @@
     return x
 
 
+def score_block(logits, target, first, out_ref):
+    count, vocab = logits.shape
+    row_max = jnp.max(logits, axis=1, keepdims=True)
+    exp_total = jnp.sum(jnp.exp(logits - row_max), axis=1, keepdims=True)
+    column = lax.broadcasted_iota(jnp.int32, (count, vocab), 1) + first
+    picked = jnp.sum(jnp.where(column == target, logits, 0.0), axis=1, keepdims=True)
+    lane = lax.broadcasted_iota(jnp.int32, (count, 128), 1)
+    packed = jnp.where(lane == 0, row_max, jnp.where(lane == 1, exp_total, picked))
+    out_ref[0] = packed.T[:8]
+
+
 def exchange_kernel(
-    shards, ways, rows_ref, weight_ref, held, got, part, w_scratch,
-    y_sems, z_sems, x_sems, c_sems, w_sems, local_sems,
+    shards, ways, rows_ref, weight_ref, target_ref, held, near, far, part, stats,
+    w_near, w_far,
+    y_sems, z_sems, x_sems, c_sems, w_sems, f_sems, local_sems,
 ):
     me = lax.axis_index("dp")
     place = lax.axis_index("mp")
@@ -52,7 +64,8 @@
     halves = ways // 2
     slots, width = rows_ref.shape
     tokens = held.shape[1]
-    vocab = got.shape[2]
+    vocab = near.shape[1]
+    cuts, _, _, cut = far.shape
 
     peers = [{"mp": flip(place, k)} for k in range(1, ways)]
     peers += [{"dp": flip(me, z * x_ways)} for z in range(1, z_ways)]
@@ -82,17 +95,26 @@
     def slot(k, r, count=1):
         return held.at[k, pl.ds(r * slots, count * slots), :]
 
-    def columns(k):
-        return weight_ref.at[:, pl.ds(pl.multiple_of(flip(place, k) * vocab, vocab), vocab)]
+    def columns(k, first=0, count=vocab):
+        start = pl.multiple_of(flip(place, k) * vocab + first, count)
+        return weight_ref.at[:, pl.ds(start, count)]
+
+    def send_far(c):
+        for k in range(2, ways):
+            far_copy[c, k] = send(
+                columns(k, c * cut, cut), far.at[c, k - 2], f_sems, c * ways + k,
+                {"mp": flip(place, k)},
+            )
 
     own_rows = pltpu.make_async_copy(rows_ref, slot(0, 0), local_sems.at[0])
     own_rows.start()
-    y_copy, z_copy, x_copy, c_copy, w_copy = {}, {}, {}, {}, {}
+    y_copy, z_copy, x_copy, c_copy, far_copy = {}, {}, {}, {}, {}
     for m in range(1, halves):
         y_copy[m] = send(rows_ref, slot(2 * m, 0), y_sems, m, {"mp": flip(place, 2 * m)})
-    for k in list(range(2, ways)) + [1]:
-        w_copy[k] = send(columns(k), got.at[k - 1], w_sems, k, {"mp": flip(place, k)})
-    own_weight = pltpu.make_async_copy(columns(0), w_scratch.at[0], local_sems.at[1])
+    for c in range(max(1, cuts - 1)):
+        send_far(c)
+    near_copy = send(columns(1), near, w_sems, 0, {"mp": flip(place, 1)})
+    own_weight = pltpu.make_async_copy(columns(0), w_near.at[0], local_sems.at[1])
     own_weight.start()
 
     def spread(m, z):
@@ -126,114 +148,98 @@
                 slot(2 * m, z * x_ways, x_ways), slot(2 * m + 1, z * x_ways, x_ways),
                 c_sems, m * z_ways + z, {"mp": flip(place, 1)},
             )
+    if cuts > 1:
+        send_far(cuts - 1)
     own_weight.wait()
-    w_copy[1].wait_recv()
-    next_weight = pltpu.make_async_copy(got.at[0], w_scratch.at[1], local_sems.at[2])
-    next_weight.start()
-    next_weight.wait()
+    near_copy.wait_recv()
+    near_weight = pltpu.make_async_copy(near, w_near.at[1], local_sems.at[2])
+    near_weight.start()
+    near_weight.wait()
     for c in c_copy.values():
         c.wait_recv()
 
+    block = 256
+    steps = (tokens // block,)
+    row_spec = pl.BlockSpec((block, width), lambda i: (i, 0))
+
     def multiply(a_ref, b_ref, out_ref):
         out_ref[...] = jnp.dot(
-            a_ref[...], w_scratch[0], preferred_element_type=jnp.float32
-        ) + jnp.dot(b_ref[...], w_scratch[1], preferred_element_type=jnp.float32)
-
-    block = 256
+            a_ref[...], w_near[0], preferred_element_type=jnp.float32
+        ) + jnp.dot(b_ref[...], w_near[1], preferred_element_type=jnp.float32)
+
     pltpu.emit_pipeline(
         multiply,
-        grid=(tokens // block,),
-        in_specs=[pl.BlockSpec((block, width), lambda i: (i, 0))] * 2,
+        grid=steps,
+        in_specs=[row_spec] * 2,
         out_specs=[pl.BlockSpec((block, vocab), lambda i: (i, 0))],
     )(held.at[0], held.at[1], part)
-    for k in range(2, ways):
-        w_copy[k].wait_recv()
+
+    for c in range(cuts):
+        for k in range(2, ways):
+            far_copy[c, k].wait_recv()
+        load = pltpu.make_async_copy(far.at[c], w_far, local_sems.at[3])
+        load.start()
+        load.wait()
+
+        def score(part_block, target_block, *refs, first=c * cut):
+            logits = part_block[...]
+            for k in range(ways - 2):
+                logits += jnp.dot(refs[k][...], w_far[k], preferred_element_type=jnp.float32)
+            score_block(logits, target_block[...], first, refs[-1])
+
+        pltpu.emit_pipeline(
+            score,
+            grid=steps,
+            in_specs=[
+                pl.BlockSpec((block, cut), functools.partial(lambda c, i: (i, c), c)),
+                pl.BlockSpec((block, 1), lambda i: (i, 0)),
+            ]
+            + [row_spec] * (ways - 2),
+            out_specs=[pl.BlockSpec((1, 8, block), functools.partial(lambda c, i: (c, 0, i), c))],
+        )(part, target_ref, *[held.at[k] for k in range(2, ways)], stats)
     for copy in started:
         copy.wait_send()
 
 
-def exchange(rows, head_weight, shards, ways):
+def score_rows(rows, head_weight, target, shards, ways):
     slots, width = rows.shape
     tokens = shards * slots
     vocab = head_weight.shape[1] // ways
     halves = ways // 2
+    cut = min(vocab, 512)
+    cuts = vocab // cut
     pairs = lambda count: pltpu.SemaphoreType.DMA((2, count))
     return pl.pallas_call(
         functools.partial(exchange_kernel, shards, ways),
-        in_specs=[pl.BlockSpec(memory_space=pl.ANY)] * 2,
-        out_specs=[pl.BlockSpec(memory_space=pl.ANY)] * 3,
+        in_specs=[pl.BlockSpec(memory_space=pl.ANY)] * 3,
+        out_specs=[pl.BlockSpec(memory_space=pl.ANY)] * 5,
         out_shape=[
             jax.ShapeDtypeStruct((ways, tokens, width), rows.dtype),
-            jax.ShapeDtypeStruct((ways - 1, width, vocab), head_weight.dtype),
+            jax.ShapeDtypeStruct((width, vocab), head_weight.dtype),
+            jax.ShapeDtypeStruct((cuts, ways - 2, width, cut), head_weight.dtype),
             jax.ShapeDtypeStruct((tokens, vocab), jnp.float32),
+            jax.ShapeDtypeStruct((cuts, 8, tokens), jnp.float32),
         ],
         scratch_shapes=[
             pltpu.VMEM((2, width, vocab), head_weight.dtype),
+            pltpu.VMEM((ways - 2, width, cut), head_weight.dtype),
             pairs(halves),
             pairs(halves * shards),
             pairs(halves * shards),
             pairs(halves * shards),
-            pairs(ways),
-            pltpu.SemaphoreType.DMA((3,)),
+            pairs(1),
+            pairs(cuts * ways),
+            pltpu.SemaphoreType.DMA((4,)),
         ],
         compiler_params=pltpu.CompilerParams(
             collective_id=0, has_side_effects=True, vmem_limit_bytes=48 * 1024 * 1024
         ),
         cost_estimate=pl.CostEstimate(
-            flops=4 * tokens * vocab * width,
-            bytes_accessed=2 * ways * width * (tokens + vocab) + 4 * tokens * vocab,
-            transcendentals=0,
-        ),
-    )(rows, head_weight)
-
-
-def score_kernel(terms, part_ref, target_ref, *refs):
-    rows = refs[:terms]
-    weights = refs[terms : 2 * terms]
-    out_ref = refs[2 * terms]
-    logits = part_ref[...]
-    for a, w in zip(rows, weights):
-        logits += jnp.dot(a[0], w[0], preferred_element_type=jnp.float32)
-    count, vocab = logits.shape
-    row_max = jnp.max(logits, axis=1, keepdims=True)
-    exp_total = jnp.sum(jnp.exp(logits - row_max), axis=1, keepdims=True)
-    column = lax.broadcasted_iota(jnp.int32, (count, vocab), 1)
-    target = jnp.sum(jnp.where(column == target_ref[...], logits, 0.0), axis=1, keepdims=True)
-    lane = lax.broadcasted_iota(jnp.int32, (count, 128), 1)
-    packed = jnp.where(lane == 0, row_max, jnp.where(lane == 1, exp_total, target))
-    out_ref[...] = packed.T[:8]
-
-
-def score_rows(part, target, held, got):
-    tokens, vocab = part.shape
-    block = 256
-    ways, _, width = held.shape
-    terms = ways - 2
-    in_specs = [
-        pl.BlockSpec((block, vocab), lambda i: (i, 0)),
-        pl.BlockSpec((block, 1), lambda i: (i, 0)),
-    ]
-    for k in range(2, ways):
-        in_specs.append(
-            pl.BlockSpec((1, block, width), functools.partial(lambda k, i: (k, i, 0), k))
-        )
-    for k in range(2, ways):
-        in_specs.append(
-            pl.BlockSpec((1, width, vocab), functools.partial(lambda k, i: (k - 1, 0, 0), k))
-        )
-    return pl.pallas_call(
-        functools.partial(score_kernel, terms),
-        grid=(tokens // block,),
-        in_specs=in_specs,
-        out_specs=pl.BlockSpec((8, block), lambda i: (0, i)),
-        out_shape=jax.ShapeDtypeStruct((8, tokens), jnp.float32),
-        compiler_params=pltpu.CompilerParams(vmem_limit_bytes=50 * 1024 * 1024),
-        cost_estimate=pl.CostEstimate(
-            flops=2 * tokens * vocab * width * terms,
-            bytes_accessed=tokens * vocab * 4 + terms * width * (tokens + vocab) * 2,
+            flops=2 * ways * tokens * vocab * width,
+            bytes_accessed=2 * ways * width * (tokens + vocab) + 8 * tokens * vocab,
             transcendentals=tokens * vocab,
         ),
-    )(part, target, *[held] * terms, *[got] * terms)
+    )(rows, head_weight, target)[4]
 
 
 def combine_stats(stats):
@@ -291,8 +297,6 @@
         ref_hidden.reshape(req_dev * max_len, width),
         preferred_element_type=jnp.float32,
     ).astype(jnp.bfloat16)
-    held, got, part = exchange(rows, head_weight, shards, ways)
-
     hidden = reward_hidden.reshape(req_dev * max_len, width).astype(jnp.float32)
     sums = jnp.stack(
         [
@@ -307,7 +311,10 @@
     ).reshape(slots)
     not_last = 1.0 - my_last.astype(jnp.float32)
     base = me * vocab_row + part_index * vocab
-    stats = score_rows(part, (targets - base).reshape(tokens, 1), held, got)[:3]
+    stats = score_rows(
+        rows, head_weight, (targets - base).reshape(tokens, 1), shards, ways
+    )
+    stats = combine_stats(stats[:, :3])
 
     stats = xor_order(stats.reshape(3, shards, shards, run), 1, me)
     sent = jnp.concatenate([stats, sums.reshape(3, 1, shards, run)], axis=1)

time: 259 us -> 247 us (0.954)
  Pallas kernels: 225 us -> 210 us
    pallas_call x2 -> x1, Pallas kernels: 225 us -> 210 us  [score_rows(): pl.pallas_call(functools.partial(exchange_kernel, shards, ways), in_specs...]
where the time goes in v3:
time: 247 us; the launch traced here: 245 us
  Pallas kernels  210 us (85%)
  local copies, waits for them, and re-layouts  10.9 us (4%)
  waiting for transfers between devices  6.16 us (2%)
  other arithmetic  6.03 us (2%)
  blocking collectives  5.19 us (2%)
  starting transfers between devices  3.89 us (2%)
    pallas_call x1, Pallas kernels, score_rows(): pl.pallas_call(functools.partial(exchange_kernel, shards, ways), in_specs...  210 us
    all_to_all x1, waiting for transfers between devices, body(): lax.all_to_all(jnp.transpose(sent, (2, 0, 1, 3)), 'dp', 0, 0, tiled=True)  6.16 us
    all_gather x1, blocking collectives, body(): gathered = lax.all_gather(jnp.concatenate([stats, sums]), 'mp')  5.19 us
  transfers between devices with their start and end apart: 1, of which 1 were waited for; matrix products, arithmetic and copies ran while one was open for 0% of the time, Pallas kernels for 0%

profile of v3, /device:TPU:0, one launch (start us, length us, event | category | flops | bytes accessed | tf_op | source)
XLA Modules:
  0.0 245.4 jit_solution(6182811650552301649)
XLA Ops:
  0.6 0.8 reshape_reshape.40
  1.4 0.8 reshape_reshape.43
  2.3 0.3 select_reduce_fusion.2
  2.6 0.1 lt.54
  2.8 0.1 lt.57
  2.9 0.2 lt.58
  3.2 0.2 eq.35
  3.5 0.2 add.86
  3.7 0.9 copy.52
  4.6 0.2 reshape_reshape.46
  4.7 0.2 rev.63
  5.0 0.7 iota_compare_fusion
  5.7 1.3 select_reduce_fusion
  7.1 0.4 copy.69
  7.5 1.7 copy.51
  9.2 1.2 reshape.189
  10.4 1.7 convolution_convert_fusion.rows_ref
  12.2 210.4 %shard_map.113 = (bf16[4,2048,1024]{2,1,0:T(8,128)(2,1)}, bf16[1024,2048]{1,0:T(8,128)(2,1)}, bf16[4,2,1024,512]{3,2,1,0:T(8,128)(2,1)}, f32[2048,2048]{1,0:T(8,128)}, f32[4,8,2048]{2,1,0:T(8,128)S(1)}) custom-call(bf16[256,1024]{1,0:T(8,128)(2,1)S(1)} %convolution_convert_fusion.rows_ref, bf16[1024,8192]{1,0:T(8,128)(2,1)} %weight_ref.1, s32[2048,1]{1,0:T(8,128)S(1)} %bitcast.86), custom_call_target="tpu_custom_call" | custom-call | flops 34359738368 | bytes 67108864 | tf_op jit(solution)/shard_map/pallas_call | solution.py:212
  222.7 0.2 copy.54
  222.9 0.5 fusion
  223.5 0.1 stack.37
  223.8 0.1 stack.38
  224.0 0.1 stack.39
  224.2 0.3 select_reduce_fusion.1
  225.0 0.7 reshape.199
  225.8 3.9 %all-to-all-start = ((f32[8,1,864]{2,1,0:T(1,128)}), f32[8,1,864]{2,1,0:T(1,128)S(1)}, u32[]{:S(2)}, u32[]{:S(2)}) async-start(f32[8,1,864]{2,1,0:T(1,128)} %reshape.199), calls=%async_computation | async-start | bytes 57344 | tf_op jit(solution)/shard_map/all_to_all | solution.py:321
  230.2 6.2 %all-to-all-done = f32[8,1,864]{2,1,0:T(1,128)S(1)} async-done(((f32[8,1,864]{2,1,0:T(1,128)}), f32[8,1,864]{2,1,0:T(1,128)S(1)}, u32[]{:S(2)}, u32[]{:S(2)}) %all-to-all-start) | async-done | bytes 27680 | tf_op jit(solution)/shard_map/all_to_all | solution.py:321
  236.3 0.5 broadcast.115
  236.8 0.7 reduce.9
  238.0 5.2 %all-gather.1 = f32[4,6,256]{2,1,0:T(8,128)S(1)} all-gather(f32[1,6,256]{2,1,0:T(8,128)S(1)} %maximum_bitcast_fusion.1), channel_id=2, replica_groups=mesh['dp'=8,'mp'=4] {'mp'}, dimensions={0}, use_global_device_ids=true | all-gather | bytes 30720 | tf_op jit(solution)/shard_map/all_gather | solution.py:324
  243.4 0.6 fusion.17
  244.8 0.6 fusion.29
  (89 shorter events, 3.3 us)
Async XLA Ops:
  12.1 210.7 %copy-start.1 = (f32[1024]{0:T(1024)S(1)}, f32[1024]{0:T(1024)}, u32[]{:S(2)}) copy-start(f32[1024]{0:T(1024)} %param.16) | copy-start | bytes 12292
  12.1 210.7 %copy-start.2 = (f32[1024]{0:T(1024)S(1)}, f32[1024]{0:T(1024)}, u32[]{:S(2)}) copy-start(f32[1024]{0:T(1024)} %param.18) | copy-start | bytes 12292
  12.1 210.7 %copy-start.3 = (f32[1024]{0:T(1024)S(1)}, f32[1024]{0:T(1024)}, u32[]{:S(2)}) copy-start(f32[1024]{0:T(1024)} %param.17) | copy-start | bytes 12292
  12.2 210.7 %copy-start = (bf16[64,7,1024]{2,0,1:T(8,128)(2,1)S(1)}, bf16[64,7,1024]{2,0,1:T(8,128)(2,1)}, u32[]{:S(2)}) copy-start(bf16[64,7,1024]{2,0,1:T(8,128)(2,1)} %param.14) | copy-start | bytes 2752516
  222.6 20.8 %copy-start.4 = (f32[256]{0:T(256)S(1)}, f32[256]{0:T(256)}, u32[]{:S(2)}) copy-start(f32[256]{0:T(256)} %param.19) | copy-start | bytes 3076
  225.8 10.6 %all-to-all-start = ((f32[8,1,864]{2,1,0:T(1,128)}), f32[8,1,864]{2,1,0:T(1,128)S(1)}, u32[]{:S(2)}, u32[]{:S(2)}) async-start(f32[8,1,864]{2,1,0:T(1,128)} %reshape.199), calls=%async_computation | async-start | bytes 57344 | tf_op jit(solution)/shard_map/all_to_all | solution.py:321

commit v4 on v3

--- a/solution.py
+++ b/solution.py
@@ -139,6 +139,8 @@
         for m in range(halves):
             z_copy[m, z].wait_recv()
             spread(m, z)
+    if cuts > 1:
+        send_far(cuts - 1)
     own_rows.wait()
     for z in range(z_ways):
         for m in range(halves):
@@ -148,8 +150,6 @@
                 slot(2 * m, z * x_ways, x_ways), slot(2 * m + 1, z * x_ways, x_ways),
                 c_sems, m * z_ways + z, {"mp": flip(place, 1)},
             )
-    if cuts > 1:
-        send_far(cuts - 1)
     own_weight.wait()
     near_copy.wait_recv()
     near_weight = pltpu.make_async_copy(near, w_near.at[1], local_sems.at[2])

time: 247 us -> 247 us (level)
  no operation moved by 1% of the time
where the time goes in v4:
time: 247 us; the launch traced here: 245 us
  Pallas kernels  210 us (85%)
  local copies, waits for them, and re-layouts  10.9 us (4%)
  waiting for transfers between devices  6.16 us (2%)
  other arithmetic  6.03 us (2%)
  blocking collectives  5.19 us (2%)
  starting transfers between devices  3.89 us (2%)
    pallas_call x1, Pallas kernels, score_rows(): pl.pallas_call(functools.partial(exchange_kernel, shards, ways), in_specs...  210 us
    all_to_all x1, waiting for transfers between devices, body(): lax.all_to_all(jnp.transpose(sent, (2, 0, 1, 3)), 'dp', 0, 0, tiled=True)  6.16 us
    all_gather x1, blocking collectives, body(): gathered = lax.all_gather(jnp.concatenate([stats, sums]), 'mp')  5.19 us
  transfers between devices with their start and end apart: 1, of which 1 were waited for; matrix products, arithmetic and copies ran while one was open for 0% of the time, Pallas kernels for 0%

profile of v4, /device:TPU:0, one launch (start us, length us, event | category | flops | bytes accessed | tf_op | source)
XLA Modules:
  0.0 245.4 jit_solution(15583015698845489798)
XLA Ops:
  0.6 0.8 reshape_reshape.40
  1.4 0.8 reshape_reshape.43
  2.3 0.3 select_reduce_fusion.2
  2.6 0.1 lt.54
  2.8 0.1 lt.57
  2.9 0.2 lt.58
  3.2 0.2 eq.35
  3.5 0.2 add.86
  3.7 0.9 copy.52
  4.6 0.2 reshape_reshape.46
  4.7 0.2 rev.63
  5.0 0.7 iota_compare_fusion
  5.7 1.3 select_reduce_fusion
  7.1 0.4 copy.69
  7.5 1.7 copy.51
  9.2 1.2 reshape.189
  10.4 1.7 convolution_convert_fusion.rows_ref
  12.2 210.4 %shard_map.113 = (bf16[4,2048,1024]{2,1,0:T(8,128)(2,1)}, bf16[1024,2048]{1,0:T(8,128)(2,1)}, bf16[4,2,1024,512]{3,2,1,0:T(8,128)(2,1)}, f32[2048,2048]{1,0:T(8,128)}, f32[4,8,2048]{2,1,0:T(8,128)S(1)}) custom-call(bf16[256,1024]{1,0:T(8,128)(2,1)S(1)} %convolution_convert_fusion.rows_ref, bf16[1024,8192]{1,0:T(8,128)(2,1)} %weight_ref.1, s32[2048,1]{1,0:T(8,128)S(1)} %bitcast.86), custom_call_target="tpu_custom_call" | custom-call | flops 34359738368 | bytes 67108864 | tf_op jit(solution)/shard_map/pallas_call | solution.py:212
  222.7 0.2 copy.54
  222.9 0.5 fusion
  223.5 0.1 stack.37
  223.8 0.1 stack.38
  224.0 0.1 stack.39
  224.2 0.3 select_reduce_fusion.1
  225.0 0.7 reshape.199
  225.8 3.9 %all-to-all-start = ((f32[8,1,864]{2,1,0:T(1,128)}), f32[8,1,864]{2,1,0:T(1,128)S(1)}, u32[]{:S(2)}, u32[]{:S(2)}) async-start(f32[8,1,864]{2,1,0:T(1,128)} %reshape.199), calls=%async_computation | async-start | bytes 57344 | tf_op jit(solution)/shard_map/all_to_all | solution.py:321
  230.2 6.2 %all-to-all-done = f32[8,1,864]{2,1,0:T(1,128)S(1)} async-done(((f32[8,1,864]{2,1,0:T(1,128)}), f32[8,1,864]{2,1,0:T(1,128)S(1)}, u32[]{:S(2)}, u32[]{:S(2)}) %all-to-all-start) | async-done | bytes 27680 | tf_op jit(solution)/shard_map/all_to_all | solution.py:321
  236.3 0.5 broadcast.115
  236.8 0.7 reduce.9
  238.0 5.2 %all-gather.1 = f32[4,6,256]{2,1,0:T(8,128)S(1)} all-gather(f32[1,6,256]{2,1,0:T(8,128)S(1)} %maximum_bitcast_fusion.1), channel_id=2, replica_groups=mesh['dp'=8,'mp'=4] {'mp'}, dimensions={0}, use_global_device_ids=true | all-gather | bytes 30720 | tf_op jit(solution)/shard_map/all_gather | solution.py:324
  243.4 0.6 fusion.17
  244.8 0.6 fusion.29
  (89 shorter events, 3.3 us)
Async XLA Ops:
  12.1 210.7 %copy-start.1 = (f32[1024]{0:T(1024)S(1)}, f32[1024]{0:T(1024)}, u32[]{:S(2)}) copy-start(f32[1024]{0:T(1024)} %param.16) | copy-start | bytes 12292
  12.1 210.7 %copy-start.2 = (f32[1024]{0:T(1024)S(1)}, f32[1024]{0:T(1024)}, u32[]{:S(2)}) copy-start(f32[1024]{0:T(1024)} %param.18) | copy-start | bytes 12292
  12.1 210.7 %copy-start.3 = (f32[1024]{0:T(1024)S(1)}, f32[1024]{0:T(1024)}, u32[]{:S(2)}) copy-start(f32[1024]{0:T(1024)} %param.17) | copy-start | bytes 12292
  12.2 210.7 %copy-start = (bf16[64,7,1024]{2,0,1:T(8,128)(2,1)S(1)}, bf16[64,7,1024]{2,0,1:T(8,128)(2,1)}, u32[]{:S(2)}) copy-start(bf16[64,7,1024]{2,0,1:T(8,128)(2,1)} %param.14) | copy-start | bytes 2752516
  222.6 20.8 %copy-start.4 = (f32[256]{0:T(256)S(1)}, f32[256]{0:T(256)}, u32[]{:S(2)}) copy-start(f32[256]{0:T(256)} %param.19) | copy-start | bytes 3076
  225.8 10.6 %all-to-all-start = ((f32[8,1,864]{2,1,0:T(1,128)}), f32[8,1,864]{2,1,0:T(1,128)S(1)}, u32[]{:S(2)}, u32[]{:S(2)}) async-start(f32[8,1,864]{2,1,0:T(1,128)} %reshape.199), calls=%async_computation | async-start | bytes 57344 | tf_op jit(solution)/shard_map/all_to_all | solution.py:321

commit v5 on v3

--- a/solution.py
+++ b/solution.py
@@ -206,7 +206,7 @@
     tokens = shards * slots
     vocab = head_weight.shape[1] // ways
     halves = ways // 2
-    cut = min(vocab, 512)
+    cut = min(vocab, 256)
     cuts = vocab // cut
     pairs = lambda count: pltpu.SemaphoreType.DMA((2, count))
     return pl.pallas_call(

time: 247 us -> 266 us (1.077)
  Pallas kernels: 210 us -> 230 us
    pallas_call x1, Pallas kernels: 210 us -> 230 us  [score_rows(): pl.pallas_call(functools.partial(exchange_kernel, shards, ways), in_specs...]
where the time goes in v5:
time: 266 us; the launch traced here: 264 us
  Pallas kernels  230 us (86%)
  local copies, waits for them, and re-layouts  11 us (4%)
  waiting for transfers between devices  6.13 us (2%)
  other arithmetic  6.09 us (2%)
  blocking collectives  5.19 us (2%)
  starting transfers between devices  3.34 us (1%)
    pallas_call x1, Pallas kernels, score_rows(): pl.pallas_call(functools.partial(exchange_kernel, shards, ways), in_specs...  230 us
    all_to_all x1, waiting for transfers between devices, body(): lax.all_to_all(jnp.transpose(sent, (2, 0, 1, 3)), 'dp', 0, 0, tiled=True)  6.13 us
  transfers between devices with their start and end apart: 1, of which 1 were waited for; matrix products, arithmetic and copies ran while one was open for 0% of the time, Pallas kernels for 0%

profile of v5, /device:TPU:0, one launch (start us, length us, event | category | flops | bytes accessed | tf_op | source)
XLA Modules:
  0.0 264.4 jit_solution(10602634289254583728)
XLA Ops:
  0.6 0.8 reshape_reshape.40
  1.4 0.8 reshape_reshape.43
  2.3 0.3 select_reduce_fusion.2
  2.6 0.1 lt.54
  2.8 0.1 lt.57
  2.9 0.2 lt.58
  3.2 0.2 eq.35
  3.5 0.2 add.86
  3.7 0.9 copy.52
  4.6 0.2 reshape_reshape.46
  4.7 0.2 rev.63
  5.0 0.7 iota_compare_fusion
  5.7 1.3 select_reduce_fusion
  7.1 0.4 copy.69
  7.5 1.7 copy.51
  9.2 1.2 reshape.189
  10.4 1.7 convolution_convert_fusion.rows_ref
  12.2 229.7 %shard_map.113 = (bf16[4,2048,1024]{2,1,0:T(8,128)(2,1)}, bf16[1024,2048]{1,0:T(8,128)(2,1)}, bf16[8,2,1024,256]{3,2,1,0:T(8,128)(2,1)}, f32[2048,2048]{1,0:T(8,128)}, f32[8,8,2048]{2,1,0:T(8,128)S(1)}) custom-call(bf16[256,1024]{1,0:T(8,128)(2,1)S(1)} %convolution_convert_fusion.rows_ref, bf16[1024,8192]{1,0:T(8,128)(2,1)} %weight_ref.1, s32[2048,1]{1,0:T(8,128)S(1)} %bitcast.86), custom_call_target="tpu_custom_call" | custom-call | flops 34359738368 | bytes 67108864 | tf_op jit(solution)/shard_map/pallas_call | solution.py:212
  242.0 0.3 copy.54
  242.4 0.5 fusion
  243.0 0.1 stack.37
  243.3 0.1 stack.38
  243.5 0.1 stack.39
  243.7 0.3 select_reduce_fusion.1
  244.6 0.7 reshape.199
  245.3 3.3 %all-to-all-start = ((f32[8,1,864]{2,1,0:T(1,128)}), f32[8,1,864]{2,1,0:T(1,128)S(1)}, u32[]{:S(2)}, u32[]{:S(2)}) async-start(f32[8,1,864]{2,1,0:T(1,128)} %reshape.199), calls=%async_computation | async-start | bytes 57344 | tf_op jit(solution)/shard_map/all_to_all | solution.py:321
  249.2 6.1 %all-to-all-done = f32[8,1,864]{2,1,0:T(1,128)S(1)} async-done(((f32[8,1,864]{2,1,0:T(1,128)}), f32[8,1,864]{2,1,0:T(1,128)S(1)}, u32[]{:S(2)}, u32[]{:S(2)}) %all-to-all-start) | async-done | bytes 27680 | tf_op jit(solution)/shard_map/all_to_all | solution.py:321
  255.3 0.5 broadcast.115
  255.8 0.7 reduce.9
  256.9 5.2 %all-gather.1 = f32[4,6,256]{2,1,0:T(8,128)S(1)} all-gather(f32[1,6,256]{2,1,0:T(8,128)S(1)} %maximum_bitcast_fusion.1), channel_id=2, replica_groups=mesh['dp'=8,'mp'=4] {'mp'}, dimensions={0}, use_global_device_ids=true | all-gather | bytes 30720 | tf_op jit(solution)/shard_map/all_gather | solution.py:324
  262.3 0.6 fusion.17
  263.7 0.6 fusion.29
  (89 shorter events, 3.3 us)
Async XLA Ops:
  12.1 230.3 %copy-start.1 = (f32[1024]{0:T(1024)S(1)}, f32[1024]{0:T(1024)}, u32[]{:S(2)}) copy-start(f32[1024]{0:T(1024)} %param.16) | copy-start | bytes 12292
  12.1 230.2 %copy-start.2 = (f32[1024]{0:T(1024)S(1)}, f32[1024]{0:T(1024)}, u32[]{:S(2)}) copy-start(f32[1024]{0:T(1024)} %param.18) | copy-start | bytes 12292
  12.1 230.2 %copy-start.3 = (f32[1024]{0:T(1024)S(1)}, f32[1024]{0:T(1024)}, u32[]{:S(2)}) copy-start(f32[1024]{0:T(1024)} %param.17) | copy-start | bytes 12292
  12.2 230.3 %copy-start = (bf16[64,7,1024]{2,0,1:T(8,128)(2,1)S(1)}, bf16[64,7,1024]{2,0,1:T(8,128)(2,1)}, u32[]{:S(2)}) copy-start(bf16[64,7,1024]{2,0,1:T(8,128)(2,1)} %param.14) | copy-start | bytes 2752516
  241.9 20.4 %copy-start.4 = (f32[256]{0:T(256)S(1)}, f32[256]{0:T(256)}, u32[]{:S(2)}) copy-start(f32[256]{0:T(256)} %param.19) | copy-start | bytes 3076
  245.3 10.0 %all-to-all-start = ((f32[8,1,864]{2,1,0:T(1,128)}), f32[8,1,864]{2,1,0:T(1,128)S(1)}, u32[]{:S(2)}, u32[]{:S(2)}) async-start(f32[8,1,864]{2,1,0:T(1,128)} %reshape.199), calls=%async_computation | async-start | bytes 57344 | tf_op jit(solution)/shard_map/all_to_all | solution.py:321
